TPU v7x, 256 devices: a whole 4x4x8 slice. The times are simulated.
256 devices in a mesh: leaf: 256 (over z, x, y, core).
Axes of the slice: x: 4, y: 4, z: 8, core: 2. Of those that a mesh axis runs over, the one named last changes fastest.
Arguments:
- points: bfloat16 [64, 524288], P(None, 'leaf'), may hold values from -6 to 6
- charges: bfloat16 [32, 524288], P(None, 'leaf'), may hold values from -0.59765625 to 0.59765625
- leaf_skel: int32 [256, 256], P('leaf'), may hold values from 0 to 2047, as said below
- up_skel: int32 [4, 256, 256], P(None, 'leaf'), may hold values from 0 to 511, as said below
- near_mask: int32 [256, 4], P('leaf'), may hold values from 0 to 1, as said below
Outputs:
- field: bfloat16 [32, 524288], P(None, 'leaf')
Inputs may be any that keep to these rules, and one draw needn't show every extreme that they name: `leaf_skel`: each row holds 256 distinct positions. Each row holds 256 distinct positions; rows of the leaves under one node of level l+1 are equal in up_skel[l]. symmetric: near_mask[i, o] equals near_mask[i+o, -o]; zero where i + o falls outside the leaves.
All inputs are finite; a program needn't handle non-finite values.
Results may differ from a plain program's by a relative error of at most 0.0055.
Values may be sent and summed in bfloat16 or wider, within the bound.
No kernel may reach another device: no remote copies, remote signals or barrier semaphores. Data moves between devices by JAX's collectives and lax.ppermute only.
A program may use at most 64 MiB of HBM per device.

v0:
```python
import functools

import jax
import jax.numpy as jnp
from jax import lax
import jax.experimental.pallas as pl
import jax.experimental.pallas.tpu as pltpu
from jax.sharding import PartitionSpec as P

f32 = jnp.float32
bf16 = jnp.bfloat16
LOG2E = 1.4426950408889634
DIM = 64
STEP = 256
PIECE = 1024
AUG = 80


def params(mib=24):
    return pltpu.CompilerParams(vmem_limit_bytes=mib * 2**20)


VM = pl.BlockSpec(memory_space=pltpu.VMEM)
SM = pl.BlockSpec(memory_space=pltpu.SMEM)
ANY = pl.BlockSpec(memory_space=pl.ANY)

SLOTS = ((2, 1), (1, 2), (0, 3), (3, 0))


def norm_parts(pts):
    wide = pts.astype(f32)
    norm = jnp.sum(wide * wide, axis=0, keepdims=True)
    high = norm.astype(bf16).astype(f32)
    rest = norm - high
    mid = rest.astype(bf16).astype(f32)
    return high, mid, rest - mid


def extra_rows(first, second, count):
    row = lax.broadcasted_iota(jnp.int32, (16, count), 0)
    out = jnp.zeros((16, count), f32)
    for place, value in enumerate(tuple(first) + tuple(second)):
        out = jnp.where(row == place, value, out)
    return out.astype(bf16)


def source_form(pts):
    ones = (1.0, 1.0, 1.0)
    return jnp.concatenate([pts, extra_rows(norm_parts(pts), ones, pts.shape[1])], axis=0)


def target_form(pts):
    inv = 1.0 / DIM
    parts = norm_parts(pts)
    scaled = (pts.astype(f32) * (2.0 * inv)).astype(bf16)
    return jnp.concatenate(
        [scaled, extra_rows((-inv, -inv, -inv), [-inv * p for p in parts], pts.shape[1])], axis=0
    )


def contract_rows(left, right):
    return lax.dot_general(left, right, (((0,), (0,)), ((), ())), preferred_element_type=f32)


def contract_cols(left, right):
    return lax.dot_general(left, right, (((1,), (1,)), ((), ())), preferred_element_type=f32)


def gauss(neg_dist):
    return jnp.exp2(neg_dist * LOG2E).astype(bf16)


def interp_t(neg_dist):
    weight = 1.0 / (1.0 - neg_dist)
    total = jnp.sum(weight, axis=0, keepdims=True)
    return (weight * (1.0 / total)).astype(bf16)


def first_kernel(out):
    out[...] = jnp.zeros_like(out)


def first():
    return pl.pallas_call(
        first_kernel,
        out_shape=jax.ShapeDtypeStruct((8, 128), f32),
        out_specs=VM,
        compiler_params=params(),
        cost_estimate=pl.CostEstimate(flops=4 * 10**9, bytes_accessed=10**6, transcendentals=0),
        name="first",
    )()


def leaf_kernel(points, charges, skel, token, weights_t, node, block):
    pts = points[...]
    block[:DIM, :] = pts
    block[DIM:, :] = charges[...]
    rank = skel.shape[1]
    spots = lax.broadcasted_iota(jnp.int32, (pts.shape[1], rank), 0)
    pick = jnp.where(spots == skel[...], 1.0, 0.0).astype(bf16)
    chosen = jnp.dot(pts, pick, preferred_element_type=f32).astype(bf16)
    weights = interp_t(contract_rows(target_form(chosen), source_form(pts)))
    weights_t[...] = weights
    node[:DIM, :] = chosen
    node[DIM:, :] = contract_cols(charges[...], weights).astype(bf16)


def leaf(points, charges, skel, token):
    rank = skel.shape[1]
    count = points.shape[1]
    rows = DIM + charges.shape[0]
    return pl.pallas_call(
        leaf_kernel,
        out_shape=(
            jax.ShapeDtypeStruct((rank, count), bf16),
            jax.ShapeDtypeStruct((rows, rank), bf16),
            jax.ShapeDtypeStruct((rows, count), bf16),
        ),
        in_specs=[VM, VM, VM, ANY],
        out_specs=(VM, VM, VM),
        compiler_params=params(),
        name="leaf",
    )(points, charges, skel, token)


def transposed(form):
    count = form.shape[1]
    pad = jnp.zeros((128 - AUG, count), f32)
    return jnp.concatenate([form.astype(f32), pad], axis=0).T.astype(bf16)


def prep_kernel(block, token, source, target):
    pts = block[:DIM, :]
    source[...] = transposed(source_form(pts))
    target[...] = target_form(pts)


def prep(block, token):
    count = block.shape[1]
    return pl.pallas_call(
        prep_kernel,
        out_shape=(
            jax.ShapeDtypeStruct((count, 128), bf16),
            jax.ShapeDtypeStruct((AUG, count), bf16),
        ),
        in_specs=[VM, ANY],
        out_specs=(VM, VM),
        compiler_params=params(),
        name="prep",
    )(block, token)


def near_columns(source, charges, target, out, first, width):
    count = source.shape[0]
    waiting = ready = None
    sums = {}

    def finish(col, src, kern):
        part = jnp.dot(charges[DIM:, src : src + PIECE], kern, preferred_element_type=f32)
        sums[col] = part if src == 0 else sums[col] + part
        if src + PIECE == count:
            out[:, col : col + STEP] = sums.pop(col)

    for col in range(0, width, STEP):
        for src in range(0, count, PIECE):
            inner = jnp.dot(
                source[src : src + PIECE, :AUG],
                target[:, first + col : first + col + STEP],
                preferred_element_type=f32,
            )
            if ready is not None:
                finish(*ready)
                ready = None
            if waiting is not None:
                ready = (waiting[0], waiting[1], gauss(waiting[2]))
            waiting = (col, src, inner)
    if ready is not None:
        finish(*ready)
    finish(waiting[0], waiting[1], gauss(waiting[2]))


def near_kernel(place, width, fresh, mask, block, *refs):
    if fresh:
        target, _, out, source = refs
    else:
        source, target, _, out = refs

    def tile():
        if fresh:
            source[...] = transposed(source_form(block[:DIM, :]))
        near_columns(source, block, target, out, width[0], width[1])

    if place is None:
        tile()
        return
    odd = lax.axis_index("leaf") % 2
    even_slot, odd_slot = SLOTS[place]
    wanted = jnp.where(odd == 1, mask[0, odd_slot], mask[0, even_slot]) > 0
    pl.when(wanted)(tile)

    @pl.when(jnp.logical_not(wanted))
    def _():
        out[...] = jnp.zeros_like(out)


def near(place, first, width, mask, block, source, target, token):
    fresh = source is None
    rows = block.shape[0] - DIM
    count = target.shape[1]
    arrays = (mask, block) + (() if fresh else (source,)) + (target, token)
    return pl.pallas_call(
        functools.partial(near_kernel, place, (first, width), fresh),
        out_shape=jax.ShapeDtypeStruct((rows, width), f32),
        in_specs=[SM] + [VM] * (len(arrays) - 2) + [ANY],
        out_specs=VM,
        scratch_shapes=[pltpu.VMEM((count, 128), bf16)] if fresh else [],
        compiler_params=params(),
        cost_estimate=pl.CostEstimate(flops=4 * 10**9 * width // count, bytes_accessed=10**6, transcendentals=0),
        name="near",
    )(*arrays)


def level_kernel(level, up, node, partner, token, half_t, parent):
    upper = (lax.axis_index("leaf") >> (level - 1)) & 1
    rank = node.shape[1]
    picks = up[level - 1]
    rows = lax.broadcasted_iota(jnp.int32, (rank, rank), 0)
    own_pick = jnp.where(rows + upper * rank == picks, 1.0, 0.0).astype(bf16)
    other_pick = jnp.where(rows + (1 - upper) * rank == picks, 1.0, 0.0).astype(bf16)
    own = node[:DIM, :]
    other = partner[:DIM, :]
    chosen = (
        jnp.dot(own, own_pick, preferred_element_type=f32)
        + jnp.dot(other, other_pick, preferred_element_type=f32)
    ).astype(bf16)
    chosen_tgt = target_form(chosen)
    own_half = interp_t(contract_rows(chosen_tgt, source_form(own)))
    other_half = interp_t(contract_rows(chosen_tgt, source_form(other)))
    half_t[...] = own_half
    charges = contract_cols(node[DIM:, :], own_half) + contract_cols(partner[DIM:, :], other_half)
    parent[:DIM, :] = chosen
    parent[DIM:, :] = charges.astype(bf16)


def climb(level, up, node, partner, token):
    rows, rank = node.shape
    return pl.pallas_call(
        functools.partial(level_kernel, level),
        out_shape=(
            jax.ShapeDtypeStruct((rank, rank), bf16),
            jax.ShapeDtypeStruct((rows, rank), bf16),
        ),
        in_specs=[VM, VM, VM, ANY],
        out_specs=(VM, VM),
        compiler_params=params(),
        name="climb",
    )(up, node, partner, token)


def couple_kernel(levels, *refs):
    for level in range(levels):
        node, partner, out = refs[level], refs[levels + level], refs[2 * levels + 1 + level]
        out[...] = coupling_of(node, partner)


def couple(nodes, partners, token):
    levels = len(nodes)
    rows, rank = nodes[0].shape
    return pl.pallas_call(
        functools.partial(couple_kernel, levels),
        out_shape=(jax.ShapeDtypeStruct((rows - DIM, rank), f32),) * levels,
        in_specs=[VM] * (2 * levels) + [ANY],
        out_specs=(VM,) * levels,
        compiler_params=params(),
        name="couple",
    )(*nodes, *partners, token)


def coupling_of(node, partner):
    kern = gauss(contract_rows(source_form(partner[:DIM, :]), target_form(node[:DIM, :])))
    return jnp.dot(partner[DIM:, :], kern, preferred_element_type=f32)


def top_kernel(levels, node, source, child, sibling, token, potential, coupling):
    place = lax.axis_index("leaf") & (2**levels - 1)
    potential[...] = jnp.where(place != 0, coupling_of(node, source), 0.0)
    coupling[...] = coupling_of(child, sibling)


def top(levels, node, source, child, sibling, token):
    rows, rank = node.shape
    return pl.pallas_call(
        functools.partial(top_kernel, levels),
        out_shape=(jax.ShapeDtypeStruct((rows - DIM, rank), f32),) * 2,
        in_specs=[VM, VM, VM, VM, ANY],
        out_specs=(VM, VM),
        compiler_params=params(),
        name="top",
    )(node, source, child, sibling, token)


def down_kernel(levels, starts, *refs):
    potential, last, weights_t = refs[:3]
    couplings = refs[3 : 3 + levels]
    halves = refs[3 + levels : 3 + 2 * levels]
    pieces = refs[3 + 2 * levels : -1]
    out = refs[-1]
    wave = potential[...] + last[...]
    for level in range(levels, 0, -1):
        wave = (
            jnp.dot(wave.astype(bf16), halves[level - 1][...], preferred_element_type=f32)
            + couplings[level - 1][...]
        )
    wave = wave.astype(bf16)
    for col in range(0, out.shape[1], STEP):
        total = None
        for start, piece in zip(starts, pieces):
            if start <= col < start + piece.shape[1]:
                part = piece[:, col - start : col - start + STEP]
                total = part if total is None else total + part
        far = jnp.dot(wave, weights_t[:, col : col + STEP], preferred_element_type=f32)
        out[:, col : col + STEP] = (total + far).astype(bf16)


def down(potential, last, weights_t, couplings, halves, pieces):
    levels = len(couplings)
    starts = [start for start, _ in pieces]
    arrays = (potential, last, weights_t, *couplings, *halves, *(p for _, p in pieces))
    return pl.pallas_call(
        functools.partial(down_kernel, levels, starts),
        out_shape=jax.ShapeDtypeStruct((potential.shape[0], weights_t.shape[1]), bf16),
        in_specs=[VM] * len(arrays),
        out_specs=VM,
        compiler_params=params(),
        name="down",
    )(*arrays)


def after(value, token):
    return lax.optimization_barrier((value, token))[0]


def top_target(i):
    core, low, high, x0 = (i >> bit & 1 for bit in range(4))
    return i ^ ((x0 | high << 1 | core << 2) << 5 | (low ^ high) << 4 or 16)


def body(points, charges, leaf_skel, up_skel, near_mask):
    levels = up_skel.shape[0]
    devices = lax.axis_size("leaf")
    pieces = []

    def send(value, target):
        pairs = [(i, target(i) % devices) for i in range(devices)]
        return lax.ppermute(value, "leaf", pairs)

    weights_t, node, block = leaf(points, charges, leaf_skel, first())
    nodes, partners, halves = [], [], []

    def exchange(mask):
        nodes.append(node)
        partners.append(send(node, lambda i: i ^ mask))

    def step(level, token):
        half_t, parent = climb(level, up_skel, nodes[-1], partners[-1], token)
        halves.append(half_t)
        return parent

    def piece(place, first_col, width, block, source, token):
        out = near(place, first_col, width, near_mask, block, source, target, token)
        pieces.append((first_col, out))
        return out

    exchange(1)
    mate = send(after(block, node), lambda i: i ^ 1)
    source, target = prep(block, node)
    node = step(1, target)
    exchange(2)
    across = send(after(block, node), lambda i: i + 1 if i % 2 else i - 1)
    token = piece(None, 0, 512, block, source, node)
    node = step(2, token)
    exchange(6)
    token = piece(None, 512, 1536, block, source, node)
    node = step(3, token)
    exchange(8)
    second = send(after(block, node), lambda i: i - 2 if i % 2 else i + 2)
    couplings = couple(nodes[:-1], partners[:-1], node)
    node = step(4, couplings[0])
    arrived = send(node, top_target)
    token = piece(0, 0, 2048, mate, None, node)
    passed = send(after(across, token), lambda i: i ^ 1)
    token = piece(1, 0, 768, across, None, token)
    wave, last_coupling = top(levels, node, arrived, nodes[-1], partners[-1], token)
    arrived = send(wave, lambda i: i ^ 1)
    wave = wave + arrived
    arrived = send(wave, lambda i: i ^ 2)
    token = piece(1, 768, 1280, across, None, wave)
    wave = wave + after(arrived, token)
    arrived = send(wave, lambda i: i ^ 6)
    token = piece(3, 0, 2048, passed, None, wave)
    wave = wave + after(arrived, token)
    arrived = send(wave, lambda i: i ^ 8)
    token = piece(2, 0, 2048, second, None, wave)
    return down(wave, arrived, weights_t, (*couplings, last_coupling), halves, pieces)


def solution(mesh):
    return jax.shard_map(
        body,
        mesh=mesh,
        in_specs=(
            P(None, "leaf"),
            P(None, "leaf"),
            P("leaf", None),
            P(None, "leaf", None),
            P("leaf", None),
        ),
        out_specs=P(None, "leaf"),
        check_vma=False,
    )
```

profile of v0, /device:TPU:36, one launch (start us, length us, event | category | flops | bytes accessed | tf_op | source)
XLA Modules:
  0.0 55.4 jit_solution(10810731345889814867)
XLA Ops:
  0.0 0.7 %copy-done.3 = s32[1,256]{1,0:T(1,128)S(1)} copy-done((s32[1,256]{1,0:T(1,128)S(1)}, s32[1,256]{1,0:T(1,128)}, u32[]{:S(2)}) %copy-start.3) | copy-done | bytes 1048
  0.7 0.2 copy-done.1
  0.9 0.1 copy-done
  1.0 1.4 %leaf.1 = (bf16[256,2048]{1,0:T(8,128)(2,1)S(1)}, bf16[96,256]{1,0:T(8,128)(2,1)S(1)}, bf16[96,2048]{1,0:T(8,128)(2,1)S(1)}) custom-call(bf16[64,2048]{1,0:T(8,128)(2,1)S(1)} %copy-done, bf16[32,2048]{1,0:T(8,128)(2,1)S(1)} %copy-done.1, s32[1,256]{1,0:T(1,128)S(1)} %copy-done.3, f32[8,128]{1,0:T(8,128)S(1)} %first.1.token), custom_call_target="tpu_custom_call" | custom-call | tf_op jit(solution)/shard_map/leaf/pallas_call | solution.py:112
  2.4 0.1 collective-permute-start
  2.5 0.5 collective-permute-start.6
  3.0 0.3 prep.1
  3.2 0.5 collective-permute-done.partner.refs_3_
  3.7 0.0 copy-done.2
  3.7 0.7 %climb.4 = (bf16[256,256]{1,0:T(8,128)(2,1)S(1)}, bf16[96,256]{1,0:T(8,128)(2,1)S(1)}) custom-call(s32[4,1,256]{2,1,0:T(1,128)S(1)} %copy-done.2, bf16[96,256]{1,0:T(8,128)(2,1)S(1)} %get-tuple-element.29.token.node.refs_0_, bf16[96,256]{1,0:T(8,128)(2,1)S(1)} %collective-permute-done.partner.refs_3_, ...), custom_call_target="tpu_custom_call" | custom-call | tf_op jit(solution)/shard_map/climb/pallas_call | solution.py:247
  4.4 0.0 copy-start.4
  4.4 1.7 %collective-permute-start.1 = (bf16[96,256]{1,0:T(8,128)(2,1)S(1)}, bf16[96,256]{1,0:T(8,128)(2,1)S(1)}, u32[]{:S(2)}, u32[]{:S(2)}) collective-permute-start(bf16[96,256]{1,0:T(8,128)(2,1)S(1)} %get-tuple-element.32.refs_2_.node.refs_1_), channel_id=1, source_target_pairs={{0,2},{1,3},{2,0},{3,1},{4,6},{5,7},{6,4},{7,5},{8,10},{9,11},{10,... | collective-permute-start | bytes 147464 | tf_op jit(solution)/shard_map/ppermute | solution.py:355
  6.1 0.0 copy-done.4
  6.1 1.5 %near.7.token.refs_11_ = f32[32,512]{1,0:T(8,128)S(1)} custom-call(s32[1,4]{1,0:T(1,128)S(1)} %copy-done.4, bf16[96,2048]{1,0:T(8,128)(2,1)S(1)} %get-tuple-element.52.block, bf16[2048,128]{1,0:T(8,128)(2,1)S(1)} %get-tuple-element.33.refs_0_, bf16[80,2048]{1,0:T(8,128)(2,1)S(1)} %get-tuple-element.31.token.refs_1_.refs_0_, ...), custom_call_target="tpu_custom_call" | custom-call | flops 1000000000 | bytes 1000000 | tf_op jit(solution)/shard_map/near/pallas_call | solution.py:211
  7.6 1.0 %collective-permute-done.1.partner.refs_4_ = bf16[96,256]{1,0:T(8,128)(2,1)S(1)} collective-permute-done((bf16[96,256]{1,0:T(8,128)(2,1)S(1)}, bf16[96,256]{1,0:T(8,128)(2,1)S(1)}, u32[]{:S(2)}, u32[]{:S(2)}) %collective-permute-start.1) | collective-permute-done | bytes 49184 | tf_op jit(solution)/shard_map/ppermute | solution.py:355
  8.6 0.7 %climb.5 = (bf16[256,256]{1,0:T(8,128)(2,1)S(1)}, bf16[96,256]{1,0:T(8,128)(2,1)S(1)}) custom-call(s32[4,1,256]{2,1,0:T(1,128)S(1)} %copy-done.2, bf16[96,256]{1,0:T(8,128)(2,1)S(1)} %get-tuple-element.32.refs_2_.node.refs_1_, bf16[96,256]{1,0:T(8,128)(2,1)S(1)} %collective-permute-done.1.partner.refs_4_, f32[32,512]{1,0:T(8,128)S(1)} %near.7.token.refs_11_), custom_call_target="tpu_custom_call" | custom-call | tf_op jit(solution)/shard_map/climb/pallas_call | solution.py:247
  9.3 3.1 %collective-permute-start.2 = (bf16[96,256]{1,0:T(8,128)(2,1)S(1)}, bf16[96,256]{1,0:T(8,128)(2,1)S(1)}, u32[]{:S(2)}, u32[]{:S(2)}) collective-permute-start(bf16[96,256]{1,0:T(8,128)(2,1)S(1)} %get-tuple-element.34.refs_2_.node), channel_id=1, source_target_pairs={{0,6},{1,7},{2,4},{3,5},{4,2},{5,3},{6,0},{7,1},{8,14},{9,15},{10,... | collective-permute-start | bytes 147464 | tf_op jit(solution)/shard_map/ppermute | solution.py:355
  12.4 3.1 %near.8.token.refs_12_ = f32[32,1536]{1,0:T(8,128)S(1)} custom-call(s32[1,4]{1,0:T(1,128)S(1)} %copy-done.4, bf16[96,2048]{1,0:T(8,128)(2,1)S(1)} %get-tuple-element.52.block, bf16[2048,128]{1,0:T(8,128)(2,1)S(1)} %get-tuple-element.33.refs_0_, bf16[80,2048]{1,0:T(8,128)(2,1)S(1)} %get-tuple-element.31.token.refs_1_.refs_0_, ...), custom_call_target="tpu_custom_call" | custom-call | flops 3000000000 | bytes 1000000 | tf_op jit(solution)/shard_map/near/pallas_call | solution.py:211
  15.5 0.0 collective-permute-done.2.partner.refs_5_
  15.5 0.7 %climb.6 = (bf16[256,256]{1,0:T(8,128)(2,1)S(1)}, bf16[96,256]{1,0:T(8,128)(2,1)S(1)}) custom-call(s32[4,1,256]{2,1,0:T(1,128)S(1)} %copy-done.2, bf16[96,256]{1,0:T(8,128)(2,1)S(1)} %get-tuple-element.34.refs_2_.node, bf16[96,256]{1,0:T(8,128)(2,1)S(1)} %collective-permute-done.2.partner.refs_5_, f32[32,1536]{1,0:T(8,128)S(1)} %near.8.token.refs_12_), custom_call_target="tpu_custom_call" | custom-call | tf_op jit(solution)/shard_map/climb/pallas_call | solution.py:247
  16.2 1.3 %collective-permute-start.3 = (bf16[96,256]{1,0:T(8,128)(2,1)S(1)}, bf16[96,256]{1,0:T(8,128)(2,1)S(1)}, u32[]{:S(2)}, u32[]{:S(2)}) collective-permute-start(bf16[96,256]{1,0:T(8,128)(2,1)S(1)} %get-tuple-element.35.refs_6_.node.child), channel_id=1, source_target_pairs={{0,8},{1,9},{2,10},{3,11},{4,12},{5,13},{6,14},{7,15},{8,0},{9,1},... | collective-permute-start | bytes 147464 | tf_op jit(solution)/shard_map/ppermute | solution.py:355
  17.4 0.0 collective-permute-start.5
  17.4 0.8 %couple.1 = (f32[32,256]{1,0:T(8,128)S(1)}, f32[32,256]{1,0:T(8,128)S(1)}, f32[32,256]{1,0:T(8,128)S(1)}) custom-call(bf16[96,256]{1,0:T(8,128)(2,1)S(1)} %get-tuple-element.29.token.node.refs_0_, bf16[96,256]{1,0:T(8,128)(2,1)S(1)} %get-tuple-element.32.refs_2_.node.refs_1_, bf16[96,256]{1,0:T(8,128)(2,1)S(1)} %get-tuple-element.34.refs_2_.node, ...), custom_call_target="tpu_custom_call" | custom-call | tf_op jit(solution)/shard_map/couple/pallas_call | solution.py:269
  18.2 2.1 %collective-permute-done.3.partner.sibling = bf16[96,256]{1,0:T(8,128)(2,1)S(1)} collective-permute-done((bf16[96,256]{1,0:T(8,128)(2,1)S(1)}, bf16[96,256]{1,0:T(8,128)(2,1)S(1)}, u32[]{:S(2)}, u32[]{:S(2)}) %collective-permute-start.3) | collective-permute-done | bytes 49184 | tf_op jit(solution)/shard_map/ppermute | solution.py:355
  20.3 0.7 %climb.7 = (bf16[256,256]{1,0:T(8,128)(2,1)S(1)}, bf16[96,256]{1,0:T(8,128)(2,1)S(1)}) custom-call(s32[4,1,256]{2,1,0:T(1,128)S(1)} %copy-done.2, bf16[96,256]{1,0:T(8,128)(2,1)S(1)} %get-tuple-element.35.refs_6_.node.child, bf16[96,256]{1,0:T(8,128)(2,1)S(1)} %collective-permute-done.3.partner.sibling, f32[32,256]{1,0:T(8,128)S(1)} %get-tuple-element.36.token.refs_3_), custom_call_target="tpu_custom_call" | custom-call | tf_op jit(solution)/shard_map/climb/pallas_call | solution.py:247
  21.0 0.6 %collective-permute-start.4 = (bf16[96,256]{1,0:T(8,128)(2,1)S(1)}, bf16[96,256]{1,0:T(8,128)(2,1)S(1)}, u32[]{:S(2)}, u32[]{:S(2)}) collective-permute-start(bf16[96,256]{1,0:T(8,128)(2,1)S(1)} %get-tuple-element.37.refs_1_.node), channel_id=1, source_target_pairs={{0,16},{1,129},{2,18},{3,147},{4,84},{5,213},{6,70},{7,199},{8,40}... | collective-permute-start | bytes 147464 | tf_op jit(solution)/shard_map/ppermute | solution.py:355
  21.6 0.0 collective-permute-done.6.block
  21.6 4.3 %near.9.refs_1_.refs_13_ = f32[32,2048]{1,0:T(8,128)S(1)} custom-call(s32[1,4]{1,0:T(1,128)S(1)} %copy-done.4, bf16[96,2048]{1,0:T(8,128)(2,1)S(1)} %collective-permute-done.6.block, bf16[80,2048]{1,0:T(8,128)(2,1)S(1)} %get-tuple-element.31.token.refs_1_.refs_0_, bf16[96,256]{1,0:T(8,128)(2,1)S(1)} %get-tuple-element.37.refs_1_.node), custom_call_target="tpu_custom_call" | custom-call | flops 4000000000 | bytes 1000000 | tf_op jit(solution)/shard_map/near/pallas_call | solution.py:211
  25.9 0.8 %collective-permute-done.5.block = bf16[96,2048]{1,0:T(8,128)(2,1)S(1)} collective-permute-done((bf16[96,2048]{1,0:T(8,128)(2,1)S(1)}, bf16[96,2048]{1,0:T(8,128)(2,1)S(1)}, u32[]{:S(2)}, u32[]{:S(2)}) %collective-permute-start.5) | collective-permute-done | bytes 393248 | tf_op jit(solution)/shard_map/ppermute | solution.py:355
  26.7 2.9 %collective-permute-start.10 = (bf16[96,2048]{1,0:T(8,128)(2,1)S(1)}, bf16[96,2048]{1,0:T(8,128)(2,1)S(1)}, u32[]{:S(2)}, u32[]{:S(2)}) collective-permute-start(bf16[96,2048]{1,0:T(8,128)(2,1)S(1)} %collective-permute-done.5.block), channel_id=1, source_target_pairs={{0,1},{1,0},{2,3},{3,2},{4,5},{5,4},{6,7},{7,6},{8,9},{9,8},{10,11... | collective-permute-start | bytes 1179656 | tf_op jit(solution)/shard_map/ppermute | solution.py:355
  29.6 2.0 %near.10.token.refs_14_ = f32[32,768]{1,0:T(8,128)S(1)} custom-call(s32[1,4]{1,0:T(1,128)S(1)} %copy-done.4, bf16[96,2048]{1,0:T(8,128)(2,1)S(1)} %collective-permute-done.5.block, bf16[80,2048]{1,0:T(8,128)(2,1)S(1)} %get-tuple-element.31.token.refs_1_.refs_0_, f32[32,2048]{1,0:T(8,128)S(1)} %near.9.refs_1_.refs_13_), custom_call_target="tpu_custom_call" | custom-call | flops 1500000000 | bytes 1000000 | tf_op jit(solution)/shard_map/near/pallas_call | solution.py:211
  31.7 0.0 collective-permute-done.4.source
  31.7 0.6 %top.1 = (f32[32,256]{1,0:T(8,128)S(1)}, f32[32,256]{1,0:T(8,128)S(1)}) custom-call(bf16[96,256]{1,0:T(8,128)(2,1)S(1)} %get-tuple-element.37.refs_1_.node, bf16[96,256]{1,0:T(8,128)(2,1)S(1)} %collective-permute-done.4.source, bf16[96,256]{1,0:T(8,128)(2,1)S(1)} %get-tuple-element.35.refs_6_.node.child, ...), custom_call_target="tpu_custom_call" | custom-call | tf_op jit(solution)/shard_map/top/pallas_call | solution.py:292
  32.3 0.0 collective-permute-start.7
  32.3 0.1 collective-permute-start.12
  32.4 1.1 %collective-permute-done.7 = f32[32,256]{1,0:T(8,128)S(1)} collective-permute-done((f32[32,256]{1,0:T(8,128)S(1)}, f32[32,256]{1,0:T(8,128)S(1)}, u32[]{:S(2)}, u32[]{:S(2)}) %collective-permute-start.7) | collective-permute-done | bytes 32800 | tf_op jit(solution)/shard_map/ppermute | solution.py:355
  33.5 1.7 %collective-permute-start.8 = (f32[32,256]{1,0:T(8,128)S(1)}, f32[32,256]{1,0:T(8,128)S(1)}, u32[]{:S(2)}, u32[]{:S(2)}) collective-permute-start(f32[32,256]{1,0:T(8,128)S(1)} %add.9.refs_1_), channel_id=1, source_target_pairs={{0,2},{1,3},{2,0},{3,1},{4,6},{5,7},{6,4},{7,5},{8,10},{9,11},{10,... | collective-permute-start | bytes 98312 | tf_op jit(solution)/shard_map/ppermute | solution.py:355
  35.2 2.9 %near.11.refs_15_ = f32[32,1280]{1,0:T(8,128)S(1)} custom-call(s32[1,4]{1,0:T(1,128)S(1)} %copy-done.4, bf16[96,2048]{1,0:T(8,128)(2,1)S(1)} %collective-permute-done.5.block, bf16[80,2048]{1,0:T(8,128)(2,1)S(1)} %get-tuple-element.31.token.refs_1_.refs_0_, f32[32,256]{1,0:T(8,128)S(1)} %add.9.refs_1_), custom_call_target="tpu_custom_call" | custom-call | flops 2500000000 | bytes 1000000 | tf_op jit(solution)/shard_map/near/pallas_call | solution.py:211
  38.1 0.3 collective-permute-done.8
  38.4 3.8 %collective-permute-start.9 = (f32[32,256]{1,0:T(8,128)S(1)}, f32[32,256]{1,0:T(8,128)S(1)}, u32[]{:S(2)}, u32[]{:S(2)}) collective-permute-start(f32[32,256]{1,0:T(8,128)S(1)} %add.10.refs_1_), channel_id=1, source_target_pairs={{0,6},{1,7},{2,4},{3,5},{4,2},{5,3},{6,0},{7,1},{8,14},{9,15},{10,... | collective-permute-start | bytes 98312 | tf_op jit(solution)/shard_map/ppermute | solution.py:355
  42.2 0.0 collective-permute-done.10.block
  42.2 0.8 %near.12.refs_16_ = f32[32,2048]{1,0:T(8,128)S(1)} custom-call(s32[1,4]{1,0:T(1,128)S(1)} %copy-done.4, bf16[96,2048]{1,0:T(8,128)(2,1)S(1)} %collective-permute-done.10.block, bf16[80,2048]{1,0:T(8,128)(2,1)S(1)} %get-tuple-element.31.token.refs_1_.refs_0_, f32[32,256]{1,0:T(8,128)S(1)} %add.10.refs_1_), custom_call_target="tpu_custom_call" | custom-call | flops 4000000000 | bytes 1000000 | tf_op jit(solution)/shard_map/near/pallas_call | solution.py:211
  43.0 1.1 %collective-permute-done.9 = f32[32,256]{1,0:T(8,128)S(1)} collective-permute-done((f32[32,256]{1,0:T(8,128)S(1)}, f32[32,256]{1,0:T(8,128)S(1)}, u32[]{:S(2)}, u32[]{:S(2)}) %collective-permute-start.9) | collective-permute-done | bytes 32800 | tf_op jit(solution)/shard_map/ppermute | solution.py:355
  44.1 5.7 %collective-permute-start.11 = (f32[32,256]{1,0:T(8,128)S(1)}, f32[32,256]{1,0:T(8,128)S(1)}, u32[]{:S(2)}, u32[]{:S(2)}) collective-permute-start(f32[32,256]{1,0:T(8,128)S(1)} %add.11.refs_1_.refs_0_), channel_id=1, source_target_pairs={{0,8},{1,9},{2,10},{3,11},{4,12},{5,13},{6,14},{7,15},{8,0},{9,1},... | collective-permute-start | bytes 98312 | tf_op jit(solution)/shard_map/ppermute | solution.py:355
  49.8 0.0 collective-permute-done.12.block
  49.8 4.1 %near.13.refs_17_ = f32[32,2048]{1,0:T(8,128)S(1)} custom-call(s32[1,4]{1,0:T(1,128)S(1)} %copy-done.4, bf16[96,2048]{1,0:T(8,128)(2,1)S(1)} %collective-permute-done.12.block, bf16[80,2048]{1,0:T(8,128)(2,1)S(1)} %get-tuple-element.31.token.refs_1_.refs_0_, f32[32,256]{1,0:T(8,128)S(1)} %add.11.refs_1_.refs_0_), custom_call_target="tpu_custom_call" | custom-call | flops 4000000000 | bytes 1000000 | tf_op jit(solution)/shard_map/near/pallas_call | solution.py:211
  53.9 0.0 collective-permute-done.11.refs_1_
  54.0 1.4 %down.1 = bf16[32,2048]{1,0:T(8,128)(2,1)} custom-call(f32[32,256]{1,0:T(8,128)S(1)} %add.11.refs_1_.refs_0_, f32[32,256]{1,0:T(8,128)S(1)} %collective-permute-done.11.refs_1_, bf16[256,2048]{1,0:T(8,128)(2,1)S(1)} %get-tuple-element.44.refs_2_, f32[32,256]{1,0:T(8,128)S(1)} %get-tuple-element.36.token.refs_3_, f32[32,256]{1,0:T(8,128)S(1)} %get-tuple-element.45.refs_4_, ...), custom_call_target="tpu_custom_call" | custom-call | tf_op jit(solution)/shard_map/down/pallas_call | solution.py:329
  (8 shorter events, 0.0 us)
Async XLA Ops:
  0.0 0.7 %copy-start.3 = (s32[1,256]{1,0:T(1,128)S(1)}, s32[1,256]{1,0:T(1,128)}, u32[]{:S(2)}) copy-start(s32[1,256]{1,0:T(1,128)} %skel.1) | copy-start | bytes 3076
  0.0 0.9 %copy-start.1 = (bf16[32,2048]{1,0:T(8,128)(2,1)S(1)}, bf16[32,2048]{1,0:T(8,128)(2,1)}, u32[]{:S(2)}) copy-start(bf16[32,2048]{1,0:T(8,128)(2,1)} %charges.1) | copy-start | bytes 393220
  0.0 1.0 %copy-start = (bf16[64,2048]{1,0:T(8,128)(2,1)S(1)}, bf16[64,2048]{1,0:T(8,128)(2,1)}, u32[]{:S(2)}) copy-start(bf16[64,2048]{1,0:T(8,128)(2,1)} %points.1) | copy-start | bytes 786436
  2.4 1.3 %collective-permute-start = (bf16[96,256]{1,0:T(8,128)(2,1)S(1)}, bf16[96,256]{1,0:T(8,128)(2,1)S(1)}, u32[]{:S(2)}, u32[]{:S(2)}) collective-permute-start(bf16[96,256]{1,0:T(8,128)(2,1)S(1)} %get-tuple-element.29.token.node.refs_0_), channel_id=1, source_target_pairs={{0,1},{1,0},{2,3},{3,2},{4,5},{5,4},{6,7},{7,6},{8,9},{9,8},{10,11... | collective-permute-start | bytes 147464 | tf_op jit(solution)/shard_map/ppermute | solution.py:355
  2.5 19.1 %collective-permute-start.6 = (bf16[96,2048]{1,0:T(8,128)(2,1)S(1)}, bf16[96,2048]{1,0:T(8,128)(2,1)S(1)}, u32[]{:S(2)}, u32[]{:S(2)}) collective-permute-start(bf16[96,2048]{1,0:T(8,128)(2,1)S(1)} %get-tuple-element.52.block), channel_id=1, source_target_pairs={{0,1},{1,0},{2,3},{3,2},{4,5},{5,4},{6,7},{7,6},{8,9},{9,8},{10,11... | collective-permute-start | bytes 1179656 | tf_op jit(solution)/shard_map/ppermute | solution.py:355
  3.0 0.7 %copy-start.2 = (s32[4,1,256]{2,1,0:T(1,128)S(1)}, s32[4,1,256]{2,1,0:T(1,128)}, u32[]{:S(2)}) copy-start(s32[4,1,256]{2,1,0:T(1,128)} %up.7) | copy-start | bytes 12292
  4.4 1.7 %copy-start.4 = (s32[1,4]{1,0:T(1,128)S(1)}, s32[1,4]{1,0:T(1,128)}, u32[]{:S(2)}) copy-start(s32[1,4]{1,0:T(1,128)} %mask.13) | copy-start | bytes 52
  4.4 4.2 %collective-permute-start.1 = (bf16[96,256]{1,0:T(8,128)(2,1)S(1)}, bf16[96,256]{1,0:T(8,128)(2,1)S(1)}, u32[]{:S(2)}, u32[]{:S(2)}) collective-permute-start(bf16[96,256]{1,0:T(8,128)(2,1)S(1)} %get-tuple-element.32.refs_2_.node.refs_1_), channel_id=1, source_target_pairs={{0,2},{1,3},{2,0},{3,1},{4,6},{5,7},{6,4},{7,5},{8,10},{9,11},{10,... | collective-permute-start | bytes 147464 | tf_op jit(solution)/shard_map/ppermute | solution.py:355
  9.3 6.2 %collective-permute-start.2 = (bf16[96,256]{1,0:T(8,128)(2,1)S(1)}, bf16[96,256]{1,0:T(8,128)(2,1)S(1)}, u32[]{:S(2)}, u32[]{:S(2)}) collective-permute-start(bf16[96,256]{1,0:T(8,128)(2,1)S(1)} %get-tuple-element.34.refs_2_.node), channel_id=1, source_target_pairs={{0,6},{1,7},{2,4},{3,5},{4,2},{5,3},{6,0},{7,1},{8,14},{9,15},{10,... | collective-permute-start | bytes 147464 | tf_op jit(solution)/shard_map/ppermute | solution.py:355
  16.2 4.2 %collective-permute-start.3 = (bf16[96,256]{1,0:T(8,128)(2,1)S(1)}, bf16[96,256]{1,0:T(8,128)(2,1)S(1)}, u32[]{:S(2)}, u32[]{:S(2)}) collective-permute-start(bf16[96,256]{1,0:T(8,128)(2,1)S(1)} %get-tuple-element.35.refs_6_.node.child), channel_id=1, source_target_pairs={{0,8},{1,9},{2,10},{3,11},{4,12},{5,13},{6,14},{7,15},{8,0},{9,1},... | collective-permute-start | bytes 147464 | tf_op jit(solution)/shard_map/ppermute | solution.py:355
  17.4 9.3 %collective-permute-start.5 = (bf16[96,2048]{1,0:T(8,128)(2,1)S(1)}, bf16[96,2048]{1,0:T(8,128)(2,1)S(1)}, u32[]{:S(2)}, u32[]{:S(2)}) collective-permute-start(bf16[96,2048]{1,0:T(8,128)(2,1)S(1)} %get-tuple-element.52.block), channel_id=1, source_target_pairs={{0,255},{1,2},{2,1},{3,4},{4,3},{5,6},{6,5},{7,8},{8,7},{9,10},{10... | collective-permute-start | bytes 1179656 | tf_op jit(solution)/shard_map/ppermute | solution.py:355
  21.0 10.7 %collective-permute-start.4 = (bf16[96,256]{1,0:T(8,128)(2,1)S(1)}, bf16[96,256]{1,0:T(8,128)(2,1)S(1)}, u32[]{:S(2)}, u32[]{:S(2)}) collective-permute-start(bf16[96,256]{1,0:T(8,128)(2,1)S(1)} %get-tuple-element.37.refs_1_.node), channel_id=1, source_target_pairs={{0,16},{1,129},{2,18},{3,147},{4,84},{5,213},{6,70},{7,199},{8,40}... | collective-permute-start | bytes 147464 | tf_op jit(solution)/shard_map/ppermute | solution.py:355
  26.7 15.4 %collective-permute-start.10 = (bf16[96,2048]{1,0:T(8,128)(2,1)S(1)}, bf16[96,2048]{1,0:T(8,128)(2,1)S(1)}, u32[]{:S(2)}, u32[]{:S(2)}) collective-permute-start(bf16[96,2048]{1,0:T(8,128)(2,1)S(1)} %collective-permute-done.5.block), channel_id=1, source_target_pairs={{0,1},{1,0},{2,3},{3,2},{4,5},{5,4},{6,7},{7,6},{8,9},{9,8},{10,11... | collective-permute-start | bytes 1179656 | tf_op jit(solution)/shard_map/ppermute | solution.py:355
  32.3 1.2 %collective-permute-start.7 = (f32[32,256]{1,0:T(8,128)S(1)}, f32[32,256]{1,0:T(8,128)S(1)}, u32[]{:S(2)}, u32[]{:S(2)}) collective-permute-start(f32[32,256]{1,0:T(8,128)S(1)} %get-tuple-element.40), channel_id=1, source_target_pairs={{0,1},{1,0},{2,3},{3,2},{4,5},{5,4},{6,7},{7,6},{8,9},{9,8},{10,11... | collective-permute-start | bytes 98312 | tf_op jit(solution)/shard_map/ppermute | solution.py:355
  32.3 17.5 %collective-permute-start.12 = (bf16[96,2048]{1,0:T(8,128)(2,1)S(1)}, bf16[96,2048]{1,0:T(8,128)(2,1)S(1)}, u32[]{:S(2)}, u32[]{:S(2)}) collective-permute-start(bf16[96,2048]{1,0:T(8,128)(2,1)S(1)} %get-tuple-element.52.block), channel_id=1, source_target_pairs={{0,2},{1,255},{2,4},{3,1},{4,6},{5,3},{6,8},{7,5},{8,10},{9,7},{10... | collective-permute-start | bytes 1179656 | tf_op jit(solution)/shard_map/ppermute | solution.py:355
  33.5 4.9 %collective-permute-start.8 = (f32[32,256]{1,0:T(8,128)S(1)}, f32[32,256]{1,0:T(8,128)S(1)}, u32[]{:S(2)}, u32[]{:S(2)}) collective-permute-start(f32[32,256]{1,0:T(8,128)S(1)} %add.9.refs_1_), channel_id=1, source_target_pairs={{0,2},{1,3},{2,0},{3,1},{4,6},{5,7},{6,4},{7,5},{8,10},{9,11},{10,... | collective-permute-start | bytes 98312 | tf_op jit(solution)/shard_map/ppermute | solution.py:355
  38.4 5.7 %collective-permute-start.9 = (f32[32,256]{1,0:T(8,128)S(1)}, f32[32,256]{1,0:T(8,128)S(1)}, u32[]{:S(2)}, u32[]{:S(2)}) collective-permute-start(f32[32,256]{1,0:T(8,128)S(1)} %add.10.refs_1_), channel_id=1, source_target_pairs={{0,6},{1,7},{2,4},{3,5},{4,2},{5,3},{6,0},{7,1},{8,14},{9,15},{10,... | collective-permute-start | bytes 98312 | tf_op jit(solution)/shard_map/ppermute | solution.py:355
  44.1 9.9 %collective-permute-start.11 = (f32[32,256]{1,0:T(8,128)S(1)}, f32[32,256]{1,0:T(8,128)S(1)}, u32[]{:S(2)}, u32[]{:S(2)}) collective-permute-start(f32[32,256]{1,0:T(8,128)S(1)} %add.11.refs_1_.refs_0_), channel_id=1, source_target_pairs={{0,8},{1,9},{2,10},{3,11},{4,12},{5,13},{6,14},{7,15},{8,0},{9,1},... | collective-permute-start | bytes 98312 | tf_op jit(solution)/shard_map/ppermute | solution.py:355
where the time goes:
time: 55.3 us; the launch traced here: 55.4 us
  Pallas kernels  25.8 us (47%)
  starting transfers between devices  21.5 us (39%)
  waiting for transfers between devices  6.96 us (13%)
  local copies, waits for them, and re-layouts  1.03 us (2%)
    ppermute x13, starting transfers between devices, send(): return lax.ppermute(value, 'leaf', pairs)  21.5 us
    pallas_call x7, Pallas kernels, near(): pl.pallas_call(functools.partial(near_kernel, place, (first, width), fres...  18.7 us
    ppermute x13, waiting for transfers between devices, send(): return lax.ppermute(value, 'leaf', pairs)  6.96 us
    pallas_call x4, Pallas kernels, climb(): pl.pallas_call(functools.partial(level_kernel, level), out_shape=(jax.Sha...  2.67 us
    pallas_call x1, Pallas kernels, down(): pl.pallas_call(functools.partial(down_kernel, levels, starts), out_shape=...  1.43 us
    pallas_call x1, Pallas kernels, leaf(): pl.pallas_call(leaf_kernel, out_shape=(jax.ShapeDtypeStruct((rank, count)...  1.36 us
  transfers between devices with their start and end apart: 13, of which 7 were waited for; matrix products, arithmetic and copies ran while one was open for 0% of the time, Pallas kernels for 41%

commit v1 on v0

--- a/solution.py
+++ b/solution.py
@@ -218,6 +218,44 @@
         cost_estimate=pl.CostEstimate(flops=4 * 10**9 * width // count, bytes_accessed=10**6, transcendentals=0),
         name="near",
     )(*arrays)
+
+
+def self_kernel(block, source, target, token, out):
+    count = source.shape[0]
+    waiting = ready = None
+
+    def finish(start, kern):
+        part = jnp.dot(block[DIM:, start : start + STEP], kern, preferred_element_type=f32)
+        out[:, start:] = part if start == 0 else out[:, start:] + part
+        if start + STEP < count:
+            out[:, start : start + STEP] += contract_cols(block[DIM:, start + STEP :], kern[:, STEP:])
+
+    for start in range(0, count, STEP):
+        inner = jnp.dot(
+            source[start : start + STEP, :AUG], target[:, start:], preferred_element_type=f32
+        )
+        if ready is not None:
+            finish(*ready)
+            ready = None
+        if waiting is not None:
+            ready = (waiting[0], gauss(waiting[1]))
+        waiting = (start, inner)
+    if ready is not None:
+        finish(*ready)
+    finish(waiting[0], gauss(waiting[1]))
+
+
+def near_self(block, source, target, token):
+    count = source.shape[0]
+    return pl.pallas_call(
+        self_kernel,
+        out_shape=jax.ShapeDtypeStruct((block.shape[0] - DIM, count), f32),
+        in_specs=[VM, VM, VM, ANY],
+        out_specs=VM,
+        compiler_params=params(),
+        cost_estimate=pl.CostEstimate(flops=4 * 10**9, bytes_accessed=10**6, transcendentals=0),
+        name="near_self",
+    )(block, source, target, token)
 
 
 def level_kernel(level, up, node, partner, token, half_t, parent):
@@ -258,77 +296,79 @@
 
 
 def couple_kernel(levels, *refs):
-    for level in range(levels):
-        node, partner, out = refs[level], refs[levels + level], refs[2 * levels + 1 + level]
-        out[...] = coupling_of(node, partner)
-
-
-def couple(nodes, partners, token):
+    halves, weights_t = refs[2 * levels : 3 * levels], refs[3 * levels]
+    constant, whole = refs[-2:]
+    wave = path = None
+    for level in range(levels - 1, -1, -1):
+        node, partner, half = refs[level], refs[levels + level], halves[level][...]
+        kern = gauss(contract_rows(source_form(partner[:DIM, :]), target_form(node[:DIM, :])))
+        coupling = jnp.dot(partner[DIM:, :], kern, preferred_element_type=f32)
+        if wave is None:
+            wave, path = coupling, half
+        else:
+            wave = jnp.dot(wave.astype(bf16), half, preferred_element_type=f32) + coupling
+            path = jnp.dot(path, half, preferred_element_type=f32).astype(bf16)
+    constant[...] = jnp.dot(wave.astype(bf16), weights_t[...], preferred_element_type=f32)
+    whole[...] = jnp.dot(path, weights_t[...], preferred_element_type=f32).astype(bf16)
+
+
+def couple(nodes, partners, halves, weights_t, token):
     levels = len(nodes)
     rows, rank = nodes[0].shape
+    count = weights_t.shape[1]
     return pl.pallas_call(
         functools.partial(couple_kernel, levels),
-        out_shape=(jax.ShapeDtypeStruct((rows - DIM, rank), f32),) * levels,
-        in_specs=[VM] * (2 * levels) + [ANY],
-        out_specs=(VM,) * levels,
-        compiler_params=params(),
+        out_shape=(
+            jax.ShapeDtypeStruct((rows - DIM, count), f32),
+            jax.ShapeDtypeStruct((rank, count), bf16),
+        ),
+        in_specs=[VM] * (3 * levels + 1) + [ANY],
+        out_specs=(VM, VM),
+        compiler_params=params(),
+        cost_estimate=pl.CostEstimate(flops=4 * 10**9, bytes_accessed=10**6, transcendentals=0),
         name="couple",
-    )(*nodes, *partners, token)
-
-
-def coupling_of(node, partner):
-    kern = gauss(contract_rows(source_form(partner[:DIM, :]), target_form(node[:DIM, :])))
-    return jnp.dot(partner[DIM:, :], kern, preferred_element_type=f32)
-
-
-def top_kernel(levels, node, source, child, sibling, token, potential, coupling):
+    )(*nodes, *partners, *halves, weights_t, token)
+
+
+def top_kernel(levels, node, source, token, potential):
     place = lax.axis_index("leaf") & (2**levels - 1)
-    potential[...] = jnp.where(place != 0, coupling_of(node, source), 0.0)
-    coupling[...] = coupling_of(child, sibling)
-
-
-def top(levels, node, source, child, sibling, token):
+    kern = gauss(contract_rows(source_form(source[:DIM, :]), target_form(node[:DIM, :])))
+    part = jnp.dot(source[DIM:, :], kern, preferred_element_type=f32)
+    potential[...] = jnp.where(place != 0, part, 0.0)
+
+
+def top(levels, node, source, token):
     rows, rank = node.shape
     return pl.pallas_call(
         functools.partial(top_kernel, levels),
-        out_shape=(jax.ShapeDtypeStruct((rows - DIM, rank), f32),) * 2,
-        in_specs=[VM, VM, VM, VM, ANY],
-        out_specs=(VM, VM),
+        out_shape=jax.ShapeDtypeStruct((rows - DIM, rank), f32),
+        in_specs=[VM, VM, ANY],
+        out_specs=VM,
         compiler_params=params(),
         name="top",
-    )(node, source, child, sibling, token)
-
-
-def down_kernel(levels, starts, *refs):
-    potential, last, weights_t = refs[:3]
-    couplings = refs[3 : 3 + levels]
-    halves = refs[3 + levels : 3 + 2 * levels]
-    pieces = refs[3 + 2 * levels : -1]
+    )(node, source, token)
+
+
+def down_kernel(starts, *refs):
+    potential, last, constant, whole = refs[:4]
+    pieces = refs[4:-1]
     out = refs[-1]
-    wave = potential[...] + last[...]
-    for level in range(levels, 0, -1):
-        wave = (
-            jnp.dot(wave.astype(bf16), halves[level - 1][...], preferred_element_type=f32)
-            + couplings[level - 1][...]
-        )
-    wave = wave.astype(bf16)
+    wave = (potential[...] + last[...]).astype(bf16)
     for col in range(0, out.shape[1], STEP):
-        total = None
+        total = constant[:, col : col + STEP]
         for start, piece in zip(starts, pieces):
             if start <= col < start + piece.shape[1]:
-                part = piece[:, col - start : col - start + STEP]
-                total = part if total is None else total + part
-        far = jnp.dot(wave, weights_t[:, col : col + STEP], preferred_element_type=f32)
+                total = total + piece[:, col - start : col - start + STEP]
+        far = jnp.dot(wave, whole[:, col : col + STEP], preferred_element_type=f32)
         out[:, col : col + STEP] = (total + far).astype(bf16)
 
 
-def down(potential, last, weights_t, couplings, halves, pieces):
-    levels = len(couplings)
+def down(potential, last, constant, whole, pieces):
     starts = [start for start, _ in pieces]
-    arrays = (potential, last, weights_t, *couplings, *halves, *(p for _, p in pieces))
-    return pl.pallas_call(
-        functools.partial(down_kernel, levels, starts),
-        out_shape=jax.ShapeDtypeStruct((potential.shape[0], weights_t.shape[1]), bf16),
+    arrays = (potential, last, constant, whole, *(p for _, p in pieces))
+    return pl.pallas_call(
+        functools.partial(down_kernel, starts),
+        out_shape=jax.ShapeDtypeStruct(constant.shape, bf16),
         in_specs=[VM] * len(arrays),
         out_specs=VM,
         compiler_params=params(),
@@ -376,32 +416,32 @@
     source, target = prep(block, node)
     node = step(1, target)
     exchange(2)
-    across = send(after(block, node), lambda i: i + 1 if i % 2 else i - 1)
-    token = piece(None, 0, 512, block, source, node)
+    token = near_self(block, source, target, node)
+    pieces.append((0, token))
     node = step(2, token)
     exchange(6)
-    token = piece(None, 512, 1536, block, source, node)
+    token = piece(0, 0, 2048, mate, None, node)
     node = step(3, token)
     exchange(8)
-    second = send(after(block, node), lambda i: i - 2 if i % 2 else i + 2)
-    couplings = couple(nodes[:-1], partners[:-1], node)
-    node = step(4, couplings[0])
+    sent = after(block, node)
+    across = send(sent, lambda i: i + 1 if i % 2 else i - 1)
+    second = send(sent, lambda i: i - 2 if i % 2 else i + 2)
+    node = step(4, node)
+    constant, whole = couple(nodes, partners, halves, weights_t, node)
     arrived = send(node, top_target)
-    token = piece(0, 0, 2048, mate, None, node)
-    passed = send(after(across, token), lambda i: i ^ 1)
-    token = piece(1, 0, 768, across, None, token)
-    wave, last_coupling = top(levels, node, arrived, nodes[-1], partners[-1], token)
+    passed = send(after(across, node), lambda i: i ^ 1)
+    wave = top(levels, node, arrived, constant)
     arrived = send(wave, lambda i: i ^ 1)
     wave = wave + arrived
     arrived = send(wave, lambda i: i ^ 2)
-    token = piece(1, 768, 1280, across, None, wave)
+    token = piece(1, 0, 2048, across, None, wave)
     wave = wave + after(arrived, token)
     arrived = send(wave, lambda i: i ^ 6)
-    token = piece(3, 0, 2048, passed, None, wave)
+    token = piece(2, 0, 2048, second, None, wave)
     wave = wave + after(arrived, token)
     arrived = send(wave, lambda i: i ^ 8)
-    token = piece(2, 0, 2048, second, None, wave)
-    return down(wave, arrived, weights_t, (*couplings, last_coupling), halves, pieces)
+    token = piece(3, 0, 2048, passed, None, wave)
+    return down(wave, arrived, constant, whole, pieces)
 
 
 def solution(mesh):

time: 55.3 us -> 52.9 us (0.957); the launches traced: 55.4 us -> 53.7 us
  Pallas kernels: 25.8 us -> 23.3 us
  waiting for transfers between devices: 6.96 us -> 8.19 us
    pallas_call x7 -> x4, Pallas kernels: 18.7 us -> 13.1 us  [near(): pl.pallas_call(functools.partial(near_kernel, place, (first, width), fres...]
    pallas_call x2 -> x3, Pallas kernels: 2 us -> 4.22 us  [the longest x1 2.9 us: near_self(): pl.pallas_call(self_kernel, out_shape=jax.ShapeDtypeStruct((block.shape[0...]
    ppermute x13, waiting for transfers between devices: 6.96 us -> 8.19 us  [send(): return lax.ppermute(value, 'leaf', pairs)]
    pallas_call x1, Pallas kernels: 0.76 us -> 1.69 us  [couple(): pl.pallas_call(functools.partial(couple_kernel, levels), out_shape=(jax.S...]
  transfers between devices with their start and end apart: 13 -> 13, of which waited for: 7 -> 6; matrix products, arithmetic and copies ran while one was open for 0% -> 0% of each run, Pallas kernels for 41% -> 38%
where the time goes in v1:
time: 52.9 us; the launch traced here: 53.7 us
  Pallas kernels  23.3 us (44%)
  starting transfers between devices  21 us (40%)
  waiting for transfers between devices  8.19 us (15%)
  local copies, waits for them, and re-layouts  1.03 us (2%)
    ppermute x13, starting transfers between devices, send(): return lax.ppermute(value, 'leaf', pairs)  21 us
    pallas_call x4, Pallas kernels, near(): pl.pallas_call(functools.partial(near_kernel, place, (first, width), fres...  13.1 us
    ppermute x13, waiting for transfers between devices, send(): return lax.ppermute(value, 'leaf', pairs)  8.19 us
    pallas_call x1, Pallas kernels, near_self(): pl.pallas_call(self_kernel, out_shape=jax.ShapeDtypeStruct((block.shape[0...  2.9 us
    pallas_call x4, Pallas kernels, climb(): pl.pallas_call(functools.partial(level_kernel, level), out_shape=(jax.Sha...  2.67 us
    pallas_call x1, Pallas kernels, couple(): pl.pallas_call(functools.partial(couple_kernel, levels), out_shape=(jax.S...  1.69 us
    pallas_call x1, Pallas kernels, leaf(): pl.pallas_call(leaf_kernel, out_shape=(jax.ShapeDtypeStruct((rank, count)...  1.36 us
  transfers between devices with their start and end apart: 13, of which 6 were waited for; matrix products, arithmetic and copies ran while one was open for 0% of the time, Pallas kernels for 38%

profile of v1, /device:TPU:36, one launch (start us, length us, event | category | flops | bytes accessed | tf_op | source)
XLA Modules:
  0.0 53.7 jit_solution(9061342036056009885)
XLA Ops:
  0.0 0.0 copy-start.3
  0.0 0.0 copy-start.1
  0.0 0.7 %copy-done.3 = s32[1,256]{1,0:T(1,128)S(1)} copy-done((s32[1,256]{1,0:T(1,128)S(1)}, s32[1,256]{1,0:T(1,128)}, u32[]{:S(2)}) %copy-start.3) | copy-done | bytes 1048
  0.7 0.2 copy-done.1
  0.9 0.1 copy-done
  1.0 1.4 %leaf.1 = (bf16[256,2048]{1,0:T(8,128)(2,1)S(1)}, bf16[96,256]{1,0:T(8,128)(2,1)S(1)}, bf16[96,2048]{1,0:T(8,128)(2,1)S(1)}) custom-call(bf16[64,2048]{1,0:T(8,128)(2,1)S(1)} %copy-done, bf16[32,2048]{1,0:T(8,128)(2,1)S(1)} %copy-done.1, s32[1,256]{1,0:T(1,128)S(1)} %copy-done.3, f32[8,128]{1,0:T(8,128)S(1)} %first.1.token), custom_call_target="tpu_custom_call" | custom-call | tf_op jit(solution)/shard_map/leaf/pallas_call | solution.py:112
  2.4 0.1 collective-permute-start
  2.5 0.5 collective-permute-start.3
  3.0 0.3 prep.1
  3.2 0.5 collective-permute-done.partner.refs_4_
  3.7 0.0 copy-done.2
  3.7 0.7 %climb.4 = (bf16[256,256]{1,0:T(8,128)(2,1)S(1)}, bf16[96,256]{1,0:T(8,128)(2,1)S(1)}) custom-call(s32[4,1,256]{2,1,0:T(1,128)S(1)} %copy-done.2, bf16[96,256]{1,0:T(8,128)(2,1)S(1)} %get-tuple-element.25.token.node.refs_0_, bf16[96,256]{1,0:T(8,128)(2,1)S(1)} %collective-permute-done.partner.refs_4_, bf16[80,2048]{1,0:T(8,128)(2,1)S(1)} %get-tuple-element.27.token.target.refs_0_), custom_call_target="tpu_custom_call" | custom-call | tf_op jit(solution)/shard_map/climb/pallas_call | solution.py:285
  4.4 1.7 %collective-permute-start.1 = (bf16[96,256]{1,0:T(8,128)(2,1)S(1)}, bf16[96,256]{1,0:T(8,128)(2,1)S(1)}, u32[]{:S(2)}, u32[]{:S(2)}) collective-permute-start(bf16[96,256]{1,0:T(8,128)(2,1)S(1)} %get-tuple-element.28.token.node.refs_1_), channel_id=1, source_target_pairs={{0,2},{1,3},{2,0},{3,1},{4,6},{5,7},{6,4},{7,5},{8,10},{9,11},{10,... | collective-permute-start | bytes 147464 | tf_op jit(solution)/shard_map/ppermute | solution.py:395
  6.0 2.9 %near_self.1.token.refs_4_ = f32[32,2048]{1,0:T(8,128)S(1)} custom-call(bf16[96,2048]{1,0:T(8,128)(2,1)S(1)} %get-tuple-element.40.block, bf16[2048,128]{1,0:T(8,128)(2,1)S(1)} %get-tuple-element.29.source, bf16[80,2048]{1,0:T(8,128)(2,1)S(1)} %get-tuple-element.27.token.target.refs_0_, bf16[96,256]{1,0:T(8,128)(2,1)S(1)} %get-tuple-element.28.token.node.refs_1_), custom_call_target="tpu_custom_call" | custom-call | flops 4000000000 | bytes 1000000 | tf_op jit(solution)/shard_map/near_self/pallas_call | solution.py:250
  8.9 0.0 collective-permute-done.1.partner.refs_5_
  8.9 0.7 %climb.5 = (bf16[256,256]{1,0:T(8,128)(2,1)S(1)}, bf16[96,256]{1,0:T(8,128)(2,1)S(1)}) custom-call(s32[4,1,256]{2,1,0:T(1,128)S(1)} %copy-done.2, bf16[96,256]{1,0:T(8,128)(2,1)S(1)} %get-tuple-element.28.token.node.refs_1_, bf16[96,256]{1,0:T(8,128)(2,1)S(1)} %collective-permute-done.1.partner.refs_5_, f32[32,2048]{1,0:T(8,128)S(1)} %near_self.1.token.refs_4_), custom_call_target="tpu_custom_call" | custom-call | tf_op jit(solution)/shard_map/climb/pallas_call | solution.py:285
  9.6 0.0 copy-start.4
  9.6 2.7 %collective-permute-start.2 = (bf16[96,256]{1,0:T(8,128)(2,1)S(1)}, bf16[96,256]{1,0:T(8,128)(2,1)S(1)}, u32[]{:S(2)}, u32[]{:S(2)}) collective-permute-start(bf16[96,256]{1,0:T(8,128)(2,1)S(1)} %get-tuple-element.30.refs_1_.node.refs_2_), channel_id=1, source_target_pairs={{0,6},{1,7},{2,4},{3,5},{4,2},{5,3},{6,0},{7,1},{8,14},{9,15},{10,... | collective-permute-start | bytes 147464 | tf_op jit(solution)/shard_map/ppermute | solution.py:395
  12.4 0.0 collective-permute-done.3.block
  12.4 0.0 copy-done.4
  12.4 0.6 %near.4.token.refs_5_ = f32[32,2048]{1,0:T(8,128)S(1)} custom-call(s32[1,4]{1,0:T(1,128)S(1)} %copy-done.4, bf16[96,2048]{1,0:T(8,128)(2,1)S(1)} %collective-permute-done.3.block, bf16[80,2048]{1,0:T(8,128)(2,1)S(1)} %get-tuple-element.27.token.target.refs_0_, bf16[96,256]{1,0:T(8,128)(2,1)S(1)} %get-tuple-element.30.refs_1_.node.refs_2_), custom_call_target="tpu_custom_call" | custom-call | flops 4000000000 | bytes 1000000 | tf_op jit(solution)/shard_map/near/pallas_call | solution.py:211
  12.9 2.1 %collective-permute-done.2.partner.refs_6_ = bf16[96,256]{1,0:T(8,128)(2,1)S(1)} collective-permute-done((bf16[96,256]{1,0:T(8,128)(2,1)S(1)}, bf16[96,256]{1,0:T(8,128)(2,1)S(1)}, u32[]{:S(2)}, u32[]{:S(2)}) %collective-permute-start.2) | collective-permute-done | bytes 49184 | tf_op jit(solution)/shard_map/ppermute | solution.py:395
  15.1 0.7 %climb.6 = (bf16[256,256]{1,0:T(8,128)(2,1)S(1)}, bf16[96,256]{1,0:T(8,128)(2,1)S(1)}) custom-call(s32[4,1,256]{2,1,0:T(1,128)S(1)} %copy-done.2, bf16[96,256]{1,0:T(8,128)(2,1)S(1)} %get-tuple-element.30.refs_1_.node.refs_2_, bf16[96,256]{1,0:T(8,128)(2,1)S(1)} %collective-permute-done.2.partner.refs_6_, f32[32,2048]{1,0:T(8,128)S(1)} %near.4.token.refs_5_), custom_call_target="tpu_custom_call" | custom-call | tf_op jit(solution)/shard_map/climb/pallas_call | solution.py:285
  15.7 1.3 %collective-permute-start.4 = (bf16[96,256]{1,0:T(8,128)(2,1)S(1)}, bf16[96,256]{1,0:T(8,128)(2,1)S(1)}, u32[]{:S(2)}, u32[]{:S(2)}) collective-permute-start(bf16[96,256]{1,0:T(8,128)(2,1)S(1)} %get-tuple-element.32.node.token.refs_3_), channel_id=1, source_target_pairs={{0,8},{1,9},{2,10},{3,11},{4,12},{5,13},{6,14},{7,15},{8,0},{9,1},... | collective-permute-start | bytes 147464 | tf_op jit(solution)/shard_map/ppermute | solution.py:395
  17.0 0.3 collective-permute-start.8
  17.3 2.6 %collective-permute-done.4.partner.refs_7_ = bf16[96,256]{1,0:T(8,128)(2,1)S(1)} collective-permute-done((bf16[96,256]{1,0:T(8,128)(2,1)S(1)}, bf16[96,256]{1,0:T(8,128)(2,1)S(1)}, u32[]{:S(2)}, u32[]{:S(2)}) %collective-permute-start.4) | collective-permute-done | bytes 49184 | tf_op jit(solution)/shard_map/ppermute | solution.py:395
  19.9 0.7 %climb.7 = (bf16[256,256]{1,0:T(8,128)(2,1)S(1)}, bf16[96,256]{1,0:T(8,128)(2,1)S(1)}) custom-call(s32[4,1,256]{2,1,0:T(1,128)S(1)} %copy-done.2, bf16[96,256]{1,0:T(8,128)(2,1)S(1)} %get-tuple-element.32.node.token.refs_3_, bf16[96,256]{1,0:T(8,128)(2,1)S(1)} %collective-permute-done.4.partner.refs_7_, bf16[96,256]{1,0:T(8,128)(2,1)S(1)} %get-tuple-element.32.node.token.refs_3_), custom_call_target="tpu_custom_call" | custom-call | tf_op jit(solution)/shard_map/climb/pallas_call | solution.py:285
  20.6 2.0 %collective-permute-start.5 = (bf16[96,256]{1,0:T(8,128)(2,1)S(1)}, bf16[96,256]{1,0:T(8,128)(2,1)S(1)}, u32[]{:S(2)}, u32[]{:S(2)}) collective-permute-start(bf16[96,256]{1,0:T(8,128)(2,1)S(1)} %get-tuple-element.33.refs_13_.node), channel_id=1, source_target_pairs={{0,16},{1,129},{2,18},{3,147},{4,84},{5,213},{6,70},{7,199},{8,40}... | collective-permute-start | bytes 147464 | tf_op jit(solution)/shard_map/ppermute | solution.py:395
  22.6 1.7 %couple.1 = (f32[32,2048]{1,0:T(8,128)S(1)}, bf16[256,2048]{1,0:T(8,128)(2,1)S(1)}) custom-call(bf16[96,256]{1,0:T(8,128)(2,1)S(1)} %get-tuple-element.25.token.node.refs_0_, bf16[96,256]{1,0:T(8,128)(2,1)S(1)} %get-tuple-element.28.token.node.refs_1_, bf16[96,256]{1,0:T(8,128)(2,1)S(1)} %get-tuple-element.30.refs_1_.node.refs_2_, ...), custom_call_target="tpu_custom_call" | custom-call | flops 4000000000 | bytes 1000000 | tf_op jit(solution)/shard_map/couple/pallas_call | solution.py:319
  24.3 1.9 %collective-permute-done.5.source = bf16[96,256]{1,0:T(8,128)(2,1)S(1)} collective-permute-done((bf16[96,256]{1,0:T(8,128)(2,1)S(1)}, bf16[96,256]{1,0:T(8,128)(2,1)S(1)}, u32[]{:S(2)}, u32[]{:S(2)}) %collective-permute-start.5) | collective-permute-done | bytes 49184 | tf_op jit(solution)/shard_map/ppermute | solution.py:395
  26.3 0.4 top.1
  26.6 1.6 %collective-permute-start.6 = (f32[32,256]{1,0:T(8,128)S(1)}, f32[32,256]{1,0:T(8,128)S(1)}, u32[]{:S(2)}, u32[]{:S(2)}) collective-permute-start(f32[32,256]{1,0:T(8,128)S(1)} %top.1), channel_id=1, source_target_pairs={{0,1},{1,0},{2,3},{3,2},{4,5},{5,4},{6,7},{7,6},{8,9},{9,8},{10,11... | collective-permute-start | bytes 98312 | tf_op jit(solution)/shard_map/ppermute | solution.py:395
  28.2 2.2 %collective-permute-start.10 = (bf16[96,2048]{1,0:T(8,128)(2,1)S(1)}, bf16[96,2048]{1,0:T(8,128)(2,1)S(1)}, u32[]{:S(2)}, u32[]{:S(2)}) collective-permute-start(bf16[96,2048]{1,0:T(8,128)(2,1)S(1)} %get-tuple-element.40.block), channel_id=1, source_target_pairs={{0,2},{1,255},{2,4},{3,1},{4,6},{5,3},{6,8},{7,5},{8,10},{9,7},{10... | collective-permute-start | bytes 1179656 | tf_op jit(solution)/shard_map/ppermute | solution.py:395
  30.4 0.0 collective-permute-done.6
  30.5 0.9 %collective-permute-start.7 = (f32[32,256]{1,0:T(8,128)S(1)}, f32[32,256]{1,0:T(8,128)S(1)}, u32[]{:S(2)}, u32[]{:S(2)}) collective-permute-start(f32[32,256]{1,0:T(8,128)S(1)} %add.9.refs_1_), channel_id=1, source_target_pairs={{0,2},{1,3},{2,0},{3,1},{4,6},{5,7},{6,4},{7,5},{8,10},{9,11},{10,... | collective-permute-start | bytes 98312 | tf_op jit(solution)/shard_map/ppermute | solution.py:395
  31.3 0.0 collective-permute-done.8.block
  31.3 0.1 collective-permute-start.12
  31.4 4.1 %near.5.refs_6_ = f32[32,2048]{1,0:T(8,128)S(1)} custom-call(s32[1,4]{1,0:T(1,128)S(1)} %copy-done.4, bf16[96,2048]{1,0:T(8,128)(2,1)S(1)} %collective-permute-done.8.block, bf16[80,2048]{1,0:T(8,128)(2,1)S(1)} %get-tuple-element.27.token.target.refs_0_, f32[32,256]{1,0:T(8,128)S(1)} %add.9.refs_1_), custom_call_target="tpu_custom_call" | custom-call | flops 4000000000 | bytes 1000000 | tf_op jit(solution)/shard_map/near/pallas_call | solution.py:211
  35.5 0.9 %collective-permute-done.7 = f32[32,256]{1,0:T(8,128)S(1)} collective-permute-done((f32[32,256]{1,0:T(8,128)S(1)}, f32[32,256]{1,0:T(8,128)S(1)}, u32[]{:S(2)}, u32[]{:S(2)}) %collective-permute-start.7) | collective-permute-done | bytes 32800 | tf_op jit(solution)/shard_map/ppermute | solution.py:395
  36.4 1.5 %collective-permute-start.9 = (f32[32,256]{1,0:T(8,128)S(1)}, f32[32,256]{1,0:T(8,128)S(1)}, u32[]{:S(2)}, u32[]{:S(2)}) collective-permute-start(f32[32,256]{1,0:T(8,128)S(1)} %add.10.refs_1_), channel_id=1, source_target_pairs={{0,6},{1,7},{2,4},{3,5},{4,2},{5,3},{6,0},{7,1},{8,14},{9,15},{10,... | collective-permute-start | bytes 98312 | tf_op jit(solution)/shard_map/ppermute | solution.py:395
  38.0 0.1 collective-permute-done.10.block
  38.1 4.4 %near.6.refs_7_ = f32[32,2048]{1,0:T(8,128)S(1)} custom-call(s32[1,4]{1,0:T(1,128)S(1)} %copy-done.4, bf16[96,2048]{1,0:T(8,128)(2,1)S(1)} %collective-permute-done.10.block, bf16[80,2048]{1,0:T(8,128)(2,1)S(1)} %get-tuple-element.27.token.target.refs_0_, f32[32,256]{1,0:T(8,128)S(1)} %add.10.refs_1_), custom_call_target="tpu_custom_call" | custom-call | flops 4000000000 | bytes 1000000 | tf_op jit(solution)/shard_map/near/pallas_call | solution.py:211
  42.5 0.0 collective-permute-done.9
  42.5 6.1 %collective-permute-start.11 = (f32[32,256]{1,0:T(8,128)S(1)}, f32[32,256]{1,0:T(8,128)S(1)}, u32[]{:S(2)}, u32[]{:S(2)}) collective-permute-start(f32[32,256]{1,0:T(8,128)S(1)} %add.11.refs_1_.refs_0_), channel_id=1, source_target_pairs={{0,8},{1,9},{2,10},{3,11},{4,12},{5,13},{6,14},{7,15},{8,0},{9,1},... | collective-permute-start | bytes 98312 | tf_op jit(solution)/shard_map/ppermute | solution.py:395
  48.6 0.0 collective-permute-done.12.block
  48.6 4.1 %near.7.refs_8_ = f32[32,2048]{1,0:T(8,128)S(1)} custom-call(s32[1,4]{1,0:T(1,128)S(1)} %copy-done.4, bf16[96,2048]{1,0:T(8,128)(2,1)S(1)} %collective-permute-done.12.block, bf16[80,2048]{1,0:T(8,128)(2,1)S(1)} %get-tuple-element.27.token.target.refs_0_, f32[32,256]{1,0:T(8,128)S(1)} %add.11.refs_1_.refs_0_), custom_call_target="tpu_custom_call" | custom-call | flops 4000000000 | bytes 1000000 | tf_op jit(solution)/shard_map/near/pallas_call | solution.py:211
  52.8 0.0 collective-permute-done.11.refs_1_
  52.8 1.0 %down.1 = bf16[32,2048]{1,0:T(8,128)(2,1)} custom-call(f32[32,256]{1,0:T(8,128)S(1)} %add.11.refs_1_.refs_0_, f32[32,256]{1,0:T(8,128)S(1)} %collective-permute-done.11.refs_1_, f32[32,2048]{1,0:T(8,128)S(1)} %get-tuple-element.39.token.refs_2_, bf16[256,2048]{1,0:T(8,128)(2,1)S(1)} %get-tuple-element.43.refs_3_, f32[32,2048]{1,0:T(8,128)S(1)} %near_self.1.token.refs_4_, ...), custom_call_target="tpu_custom_call" | custom-call | tf_op jit(solution)/shard_map/down/pallas_call | solution.py:369
  (6 shorter events, 0.0 us)
Async XLA Ops:
  0.0 0.7 %copy-start.3 = (s32[1,256]{1,0:T(1,128)S(1)}, s32[1,256]{1,0:T(1,128)}, u32[]{:S(2)}) copy-start(s32[1,256]{1,0:T(1,128)} %skel.1) | copy-start | bytes 3076
  0.0 0.9 %copy-start.1 = (bf16[32,2048]{1,0:T(8,128)(2,1)S(1)}, bf16[32,2048]{1,0:T(8,128)(2,1)}, u32[]{:S(2)}) copy-start(bf16[32,2048]{1,0:T(8,128)(2,1)} %charges.1) | copy-start | bytes 393220
  0.0 1.0 %copy-start = (bf16[64,2048]{1,0:T(8,128)(2,1)S(1)}, bf16[64,2048]{1,0:T(8,128)(2,1)}, u32[]{:S(2)}) copy-start(bf16[64,2048]{1,0:T(8,128)(2,1)} %points.1) | copy-start | bytes 786436
  2.4 1.3 %collective-permute-start = (bf16[96,256]{1,0:T(8,128)(2,1)S(1)}, bf16[96,256]{1,0:T(8,128)(2,1)S(1)}, u32[]{:S(2)}, u32[]{:S(2)}) collective-permute-start(bf16[96,256]{1,0:T(8,128)(2,1)S(1)} %get-tuple-element.25.token.node.refs_0_), channel_id=1, source_target_pairs={{0,1},{1,0},{2,3},{3,2},{4,5},{5,4},{6,7},{7,6},{8,9},{9,8},{10,11... | collective-permute-start | bytes 147464 | tf_op jit(solution)/shard_map/ppermute | solution.py:395
  2.5 9.9 %collective-permute-start.3 = (bf16[96,2048]{1,0:T(8,128)(2,1)S(1)}, bf16[96,2048]{1,0:T(8,128)(2,1)S(1)}, u32[]{:S(2)}, u32[]{:S(2)}) collective-permute-start(bf16[96,2048]{1,0:T(8,128)(2,1)S(1)} %get-tuple-element.40.block), channel_id=1, source_target_pairs={{0,1},{1,0},{2,3},{3,2},{4,5},{5,4},{6,7},{7,6},{8,9},{9,8},{10,11... | collective-permute-start | bytes 1179656 | tf_op jit(solution)/shard_map/ppermute | solution.py:395
  3.0 0.7 %copy-start.2 = (s32[4,1,256]{2,1,0:T(1,128)S(1)}, s32[4,1,256]{2,1,0:T(1,128)}, u32[]{:S(2)}) copy-start(s32[4,1,256]{2,1,0:T(1,128)} %up.7) | copy-start | bytes 12292
  4.4 4.6 %collective-permute-start.1 = (bf16[96,256]{1,0:T(8,128)(2,1)S(1)}, bf16[96,256]{1,0:T(8,128)(2,1)S(1)}, u32[]{:S(2)}, u32[]{:S(2)}) collective-permute-start(bf16[96,256]{1,0:T(8,128)(2,1)S(1)} %get-tuple-element.28.token.node.refs_1_), channel_id=1, source_target_pairs={{0,2},{1,3},{2,0},{3,1},{4,6},{5,7},{6,4},{7,5},{8,10},{9,11},{10,... | collective-permute-start | bytes 147464 | tf_op jit(solution)/shard_map/ppermute | solution.py:395
  9.6 2.7 %copy-start.4 = (s32[1,4]{1,0:T(1,128)S(1)}, s32[1,4]{1,0:T(1,128)}, u32[]{:S(2)}) copy-start(s32[1,4]{1,0:T(1,128)} %mask.7) | copy-start | bytes 52
  9.6 5.4 %collective-permute-start.2 = (bf16[96,256]{1,0:T(8,128)(2,1)S(1)}, bf16[96,256]{1,0:T(8,128)(2,1)S(1)}, u32[]{:S(2)}, u32[]{:S(2)}) collective-permute-start(bf16[96,256]{1,0:T(8,128)(2,1)S(1)} %get-tuple-element.30.refs_1_.node.refs_2_), channel_id=1, source_target_pairs={{0,6},{1,7},{2,4},{3,5},{4,2},{5,3},{6,0},{7,1},{8,14},{9,15},{10,... | collective-permute-start | bytes 147464 | tf_op jit(solution)/shard_map/ppermute | solution.py:395
  15.7 4.2 %collective-permute-start.4 = (bf16[96,256]{1,0:T(8,128)(2,1)S(1)}, bf16[96,256]{1,0:T(8,128)(2,1)S(1)}, u32[]{:S(2)}, u32[]{:S(2)}) collective-permute-start(bf16[96,256]{1,0:T(8,128)(2,1)S(1)} %get-tuple-element.32.node.token.refs_3_), channel_id=1, source_target_pairs={{0,8},{1,9},{2,10},{3,11},{4,12},{5,13},{6,14},{7,15},{8,0},{9,1},... | collective-permute-start | bytes 147464 | tf_op jit(solution)/shard_map/ppermute | solution.py:395
  17.0 14.3 %collective-permute-start.8 = (bf16[96,2048]{1,0:T(8,128)(2,1)S(1)}, bf16[96,2048]{1,0:T(8,128)(2,1)S(1)}, u32[]{:S(2)}, u32[]{:S(2)}) collective-permute-start(bf16[96,2048]{1,0:T(8,128)(2,1)S(1)} %get-tuple-element.40.block), channel_id=1, source_target_pairs={{0,255},{1,2},{2,1},{3,4},{4,3},{5,6},{6,5},{7,8},{8,7},{9,10},{10... | collective-permute-start | bytes 1179656 | tf_op jit(solution)/shard_map/ppermute | solution.py:395
  20.6 5.7 %collective-permute-start.5 = (bf16[96,256]{1,0:T(8,128)(2,1)S(1)}, bf16[96,256]{1,0:T(8,128)(2,1)S(1)}, u32[]{:S(2)}, u32[]{:S(2)}) collective-permute-start(bf16[96,256]{1,0:T(8,128)(2,1)S(1)} %get-tuple-element.33.refs_13_.node), channel_id=1, source_target_pairs={{0,16},{1,129},{2,18},{3,147},{4,84},{5,213},{6,70},{7,199},{8,40}... | collective-permute-start | bytes 147464 | tf_op jit(solution)/shard_map/ppermute | solution.py:395
  26.6 3.8 %collective-permute-start.6 = (f32[32,256]{1,0:T(8,128)S(1)}, f32[32,256]{1,0:T(8,128)S(1)}, u32[]{:S(2)}, u32[]{:S(2)}) collective-permute-start(f32[32,256]{1,0:T(8,128)S(1)} %top.1), channel_id=1, source_target_pairs={{0,1},{1,0},{2,3},{3,2},{4,5},{5,4},{6,7},{7,6},{8,9},{9,8},{10,11... | collective-permute-start | bytes 98312 | tf_op jit(solution)/shard_map/ppermute | solution.py:395
  28.2 9.9 %collective-permute-start.10 = (bf16[96,2048]{1,0:T(8,128)(2,1)S(1)}, bf16[96,2048]{1,0:T(8,128)(2,1)S(1)}, u32[]{:S(2)}, u32[]{:S(2)}) collective-permute-start(bf16[96,2048]{1,0:T(8,128)(2,1)S(1)} %get-tuple-element.40.block), channel_id=1, source_target_pairs={{0,2},{1,255},{2,4},{3,1},{4,6},{5,3},{6,8},{7,5},{8,10},{9,7},{10... | collective-permute-start | bytes 1179656 | tf_op jit(solution)/shard_map/ppermute | solution.py:395
  30.5 6.0 %collective-permute-start.7 = (f32[32,256]{1,0:T(8,128)S(1)}, f32[32,256]{1,0:T(8,128)S(1)}, u32[]{:S(2)}, u32[]{:S(2)}) collective-permute-start(f32[32,256]{1,0:T(8,128)S(1)} %add.9.refs_1_), channel_id=1, source_target_pairs={{0,2},{1,3},{2,0},{3,1},{4,6},{5,7},{6,4},{7,5},{8,10},{9,11},{10,... | collective-permute-start | bytes 98312 | tf_op jit(solution)/shard_map/ppermute | solution.py:395
  31.3 17.3 %collective-permute-start.12 = (bf16[96,2048]{1,0:T(8,128)(2,1)S(1)}, bf16[96,2048]{1,0:T(8,128)(2,1)S(1)}, u32[]{:S(2)}, u32[]{:S(2)}) collective-permute-start(bf16[96,2048]{1,0:T(8,128)(2,1)S(1)} %collective-permute-done.8.block), channel_id=1, source_target_pairs={{0,1},{1,0},{2,3},{3,2},{4,5},{5,4},{6,7},{7,6},{8,9},{9,8},{10,11... | collective-permute-start | bytes 1179656 | tf_op jit(solution)/shard_map/ppermute | solution.py:395
  36.4 6.0 %collective-permute-start.9 = (f32[32,256]{1,0:T(8,128)S(1)}, f32[32,256]{1,0:T(8,128)S(1)}, u32[]{:S(2)}, u32[]{:S(2)}) collective-permute-start(f32[32,256]{1,0:T(8,128)S(1)} %add.10.refs_1_), channel_id=1, source_target_pairs={{0,6},{1,7},{2,4},{3,5},{4,2},{5,3},{6,0},{7,1},{8,14},{9,15},{10,... | collective-permute-start | bytes 98312 | tf_op jit(solution)/shard_map/ppermute | solution.py:395
  42.5 10.3 %collective-permute-start.11 = (f32[32,256]{1,0:T(8,128)S(1)}, f32[32,256]{1,0:T(8,128)S(1)}, u32[]{:S(2)}, u32[]{:S(2)}) collective-permute-start(f32[32,256]{1,0:T(8,128)S(1)} %add.11.refs_1_.refs_0_), channel_id=1, source_target_pairs={{0,8},{1,9},{2,10},{3,11},{4,12},{5,13},{6,14},{7,15},{8,0},{9,1},... | collective-permute-start | bytes 98312 | tf_op jit(solution)/shard_map/ppermute | solution.py:395

commit v2 on v1

--- a/solution.py
+++ b/solution.py
@@ -215,7 +215,7 @@
         out_specs=VM,
         scratch_shapes=[pltpu.VMEM((count, 128), bf16)] if fresh else [],
         compiler_params=params(),
-        cost_estimate=pl.CostEstimate(flops=4 * 10**9 * width // count, bytes_accessed=10**6, transcendentals=0),
+        cost_estimate=pl.CostEstimate(flops=(5 if place == 3 else 40) * 10**8 * width // count, bytes_accessed=10**6, transcendentals=0),
         name="near",
     )(*arrays)
 
@@ -390,6 +390,10 @@
     devices = lax.axis_size("leaf")
     pieces = []
 
+    def two_on(i):
+        to = i - 2 if i % 2 else i + 2
+        return to if 0 <= to < devices else i ^ 1
+
     def send(value, target):
         pairs = [(i, target(i) % devices) for i in range(devices)]
         return lax.ppermute(value, "leaf", pairs)
@@ -425,7 +429,7 @@
     exchange(8)
     sent = after(block, node)
     across = send(sent, lambda i: i + 1 if i % 2 else i - 1)
-    second = send(sent, lambda i: i - 2 if i % 2 else i + 2)
+    second = send(sent, two_on)
     node = step(4, node)
     constant, whole = couple(nodes, partners, halves, weights_t, node)
     arrived = send(node, top_target)
@@ -433,14 +437,14 @@
     wave = top(levels, node, arrived, constant)
     arrived = send(wave, lambda i: i ^ 1)
     wave = wave + arrived
+    arrived = send(wave, lambda i: i ^ 8)
+    token = piece(1, 0, 2048, across, None, wave)
+    wave = wave + after(arrived, token)
     arrived = send(wave, lambda i: i ^ 2)
-    token = piece(1, 0, 2048, across, None, wave)
+    token = piece(3, 0, 2048, passed, None, wave)
     wave = wave + after(arrived, token)
     arrived = send(wave, lambda i: i ^ 6)
     token = piece(2, 0, 2048, second, None, wave)
-    wave = wave + after(arrived, token)
-    arrived = send(wave, lambda i: i ^ 8)
-    token = piece(3, 0, 2048, passed, None, wave)
     return down(wave, arrived, constant, whole, pieces)
 
 

time: 52.9 us -> 50.7 us (0.958)
  the two profiles are of different devices: /device:TPU:36 before, /device:TPU:102 now
where the time goes in v2:
time: 50.7 us; the launch traced here: 50.2 us
  Pallas kernels  23.3 us (46%)
  starting transfers between devices  19.8 us (39%)
  waiting for transfers between devices  5.87 us (12%)
  local copies, waits for them, and re-layouts  1.03 us (2%)
    ppermute x13, starting transfers between devices, send(): return lax.ppermute(value, 'leaf', pairs)  19.8 us
    pallas_call x4, Pallas kernels, near(): pl.pallas_call(functools.partial(near_kernel, place, (first, width), fres...  13.1 us
    ppermute x13, waiting for transfers between devices, send(): return lax.ppermute(value, 'leaf', pairs)  5.87 us
    pallas_call x1, Pallas kernels, near_self(): pl.pallas_call(self_kernel, out_shape=jax.ShapeDtypeStruct((block.shape[0...  2.9 us
    pallas_call x4, Pallas kernels, climb(): pl.pallas_call(functools.partial(level_kernel, level), out_shape=(jax.Sha...  2.67 us
    pallas_call x1, Pallas kernels, couple(): pl.pallas_call(functools.partial(couple_kernel, levels), out_shape=(jax.S...  1.69 us
    pallas_call x1, Pallas kernels, leaf(): pl.pallas_call(leaf_kernel, out_shape=(jax.ShapeDtypeStruct((rank, count)...  1.36 us
    unnamed x10, local copies, waits for them, and re-layouts  1.03 us
  transfers between devices with their start and end apart: 13, of which 5 were waited for; matrix products, arithmetic and copies ran while one was open for 0% of the time, Pallas kernels for 41%

profile of v2, /device:TPU:102, one launch (start us, length us, event | category | flops | bytes accessed | tf_op | source)
XLA Modules:
  0.0 50.2 jit_solution(14311328707265072560)
XLA Ops:
  0.0 0.0 copy-start.3
  0.0 0.0 copy-start.1
  0.0 0.7 %copy-done.3 = s32[1,256]{1,0:T(1,128)S(1)} copy-done((s32[1,256]{1,0:T(1,128)S(1)}, s32[1,256]{1,0:T(1,128)}, u32[]{:S(2)}) %copy-start.3) | copy-done | bytes 1048
  0.7 0.2 copy-done.1
  0.9 0.1 copy-done
  1.0 1.4 %leaf.1 = (bf16[256,2048]{1,0:T(8,128)(2,1)S(1)}, bf16[96,256]{1,0:T(8,128)(2,1)S(1)}, bf16[96,2048]{1,0:T(8,128)(2,1)S(1)}) custom-call(bf16[64,2048]{1,0:T(8,128)(2,1)S(1)} %copy-done, bf16[32,2048]{1,0:T(8,128)(2,1)S(1)} %copy-done.1, s32[1,256]{1,0:T(1,128)S(1)} %copy-done.3, f32[8,128]{1,0:T(8,128)S(1)} %first.1.token), custom_call_target="tpu_custom_call" | custom-call | tf_op jit(solution)/shard_map/leaf/pallas_call | solution.py:112
  2.4 0.1 collective-permute-start
  2.5 0.5 collective-permute-start.3
  3.0 0.3 prep.1
  3.2 0.5 collective-permute-done.partner.refs_4_
  3.7 0.0 copy-done.2
  3.7 0.7 %climb.4 = (bf16[256,256]{1,0:T(8,128)(2,1)S(1)}, bf16[96,256]{1,0:T(8,128)(2,1)S(1)}) custom-call(s32[4,1,256]{2,1,0:T(1,128)S(1)} %copy-done.2, bf16[96,256]{1,0:T(8,128)(2,1)S(1)} %get-tuple-element.25.token.node.refs_0_, bf16[96,256]{1,0:T(8,128)(2,1)S(1)} %collective-permute-done.partner.refs_4_, bf16[80,2048]{1,0:T(8,128)(2,1)S(1)} %get-tuple-element.27.token.target.refs_0_), custom_call_target="tpu_custom_call" | custom-call | tf_op jit(solution)/shard_map/climb/pallas_call | solution.py:285
  4.4 1.7 %collective-permute-start.1 = (bf16[96,256]{1,0:T(8,128)(2,1)S(1)}, bf16[96,256]{1,0:T(8,128)(2,1)S(1)}, u32[]{:S(2)}, u32[]{:S(2)}) collective-permute-start(bf16[96,256]{1,0:T(8,128)(2,1)S(1)} %get-tuple-element.28.token.node.refs_1_), channel_id=1, source_target_pairs={{0,2},{1,3},{2,0},{3,1},{4,6},{5,7},{6,4},{7,5},{8,10},{9,11},{10,... | collective-permute-start | bytes 147464 | tf_op jit(solution)/shard_map/ppermute | solution.py:399
  6.0 2.9 %near_self.1.token.refs_4_ = f32[32,2048]{1,0:T(8,128)S(1)} custom-call(bf16[96,2048]{1,0:T(8,128)(2,1)S(1)} %get-tuple-element.40.block, bf16[2048,128]{1,0:T(8,128)(2,1)S(1)} %get-tuple-element.29.source, bf16[80,2048]{1,0:T(8,128)(2,1)S(1)} %get-tuple-element.27.token.target.refs_0_, bf16[96,256]{1,0:T(8,128)(2,1)S(1)} %get-tuple-element.28.token.node.refs_1_), custom_call_target="tpu_custom_call" | custom-call | flops 4000000000 | bytes 1000000 | tf_op jit(solution)/shard_map/near_self/pallas_call | solution.py:250
  8.9 0.0 collective-permute-done.1.partner.refs_5_
  8.9 0.7 %climb.5 = (bf16[256,256]{1,0:T(8,128)(2,1)S(1)}, bf16[96,256]{1,0:T(8,128)(2,1)S(1)}) custom-call(s32[4,1,256]{2,1,0:T(1,128)S(1)} %copy-done.2, bf16[96,256]{1,0:T(8,128)(2,1)S(1)} %get-tuple-element.28.token.node.refs_1_, bf16[96,256]{1,0:T(8,128)(2,1)S(1)} %collective-permute-done.1.partner.refs_5_, f32[32,2048]{1,0:T(8,128)S(1)} %near_self.1.token.refs_4_), custom_call_target="tpu_custom_call" | custom-call | tf_op jit(solution)/shard_map/climb/pallas_call | solution.py:285
  9.6 0.0 copy-start.4
  9.6 2.7 %collective-permute-start.2 = (bf16[96,256]{1,0:T(8,128)(2,1)S(1)}, bf16[96,256]{1,0:T(8,128)(2,1)S(1)}, u32[]{:S(2)}, u32[]{:S(2)}) collective-permute-start(bf16[96,256]{1,0:T(8,128)(2,1)S(1)} %get-tuple-element.30.refs_1_.node.refs_2_), channel_id=1, source_target_pairs={{0,6},{1,7},{2,4},{3,5},{4,2},{5,3},{6,0},{7,1},{8,14},{9,15},{10,... | collective-permute-start | bytes 147464 | tf_op jit(solution)/shard_map/ppermute | solution.py:399
  12.4 0.0 collective-permute-done.3.block
  12.4 0.0 copy-done.4
  12.4 0.6 %near.4.token.refs_5_ = f32[32,2048]{1,0:T(8,128)S(1)} custom-call(s32[1,4]{1,0:T(1,128)S(1)} %copy-done.4, bf16[96,2048]{1,0:T(8,128)(2,1)S(1)} %collective-permute-done.3.block, bf16[80,2048]{1,0:T(8,128)(2,1)S(1)} %get-tuple-element.27.token.target.refs_0_, bf16[96,256]{1,0:T(8,128)(2,1)S(1)} %get-tuple-element.30.refs_1_.node.refs_2_), custom_call_target="tpu_custom_call" | custom-call | flops 4000000000 | bytes 1000000 | tf_op jit(solution)/shard_map/near/pallas_call | solution.py:211
  12.9 2.1 %collective-permute-done.2.partner.refs_6_ = bf16[96,256]{1,0:T(8,128)(2,1)S(1)} collective-permute-done((bf16[96,256]{1,0:T(8,128)(2,1)S(1)}, bf16[96,256]{1,0:T(8,128)(2,1)S(1)}, u32[]{:S(2)}, u32[]{:S(2)}) %collective-permute-start.2) | collective-permute-done | bytes 49184 | tf_op jit(solution)/shard_map/ppermute | solution.py:399
  15.1 0.7 %climb.6 = (bf16[256,256]{1,0:T(8,128)(2,1)S(1)}, bf16[96,256]{1,0:T(8,128)(2,1)S(1)}) custom-call(s32[4,1,256]{2,1,0:T(1,128)S(1)} %copy-done.2, bf16[96,256]{1,0:T(8,128)(2,1)S(1)} %get-tuple-element.30.refs_1_.node.refs_2_, bf16[96,256]{1,0:T(8,128)(2,1)S(1)} %collective-permute-done.2.partner.refs_6_, f32[32,2048]{1,0:T(8,128)S(1)} %near.4.token.refs_5_), custom_call_target="tpu_custom_call" | custom-call | tf_op jit(solution)/shard_map/climb/pallas_call | solution.py:285
  15.7 0.9 %collective-permute-start.4 = (bf16[96,256]{1,0:T(8,128)(2,1)S(1)}, bf16[96,256]{1,0:T(8,128)(2,1)S(1)}, u32[]{:S(2)}, u32[]{:S(2)}) collective-permute-start(bf16[96,256]{1,0:T(8,128)(2,1)S(1)} %get-tuple-element.32.node.token.refs_3_), channel_id=1, source_target_pairs={{0,8},{1,9},{2,10},{3,11},{4,12},{5,13},{6,14},{7,15},{8,0},{9,1},... | collective-permute-start | bytes 147464 | tf_op jit(solution)/shard_map/ppermute | solution.py:399
  16.6 1.0 %collective-permute-start.8 = (bf16[96,2048]{1,0:T(8,128)(2,1)S(1)}, bf16[96,2048]{1,0:T(8,128)(2,1)S(1)}, u32[]{:S(2)}, u32[]{:S(2)}) collective-permute-start(bf16[96,2048]{1,0:T(8,128)(2,1)S(1)} %get-tuple-element.40.block), channel_id=1, source_target_pairs={{0,255},{1,2},{2,1},{3,4},{4,3},{5,6},{6,5},{7,8},{8,7},{9,10},{10... | collective-permute-start | bytes 1179656 | tf_op jit(solution)/shard_map/ppermute | solution.py:399
  17.6 2.3 %collective-permute-done.4.partner.refs_7_ = bf16[96,256]{1,0:T(8,128)(2,1)S(1)} collective-permute-done((bf16[96,256]{1,0:T(8,128)(2,1)S(1)}, bf16[96,256]{1,0:T(8,128)(2,1)S(1)}, u32[]{:S(2)}, u32[]{:S(2)}) %collective-permute-start.4) | collective-permute-done | bytes 49184 | tf_op jit(solution)/shard_map/ppermute | solution.py:399
  19.9 0.7 %climb.7 = (bf16[256,256]{1,0:T(8,128)(2,1)S(1)}, bf16[96,256]{1,0:T(8,128)(2,1)S(1)}) custom-call(s32[4,1,256]{2,1,0:T(1,128)S(1)} %copy-done.2, bf16[96,256]{1,0:T(8,128)(2,1)S(1)} %get-tuple-element.32.node.token.refs_3_, bf16[96,256]{1,0:T(8,128)(2,1)S(1)} %collective-permute-done.4.partner.refs_7_, bf16[96,256]{1,0:T(8,128)(2,1)S(1)} %get-tuple-element.32.node.token.refs_3_), custom_call_target="tpu_custom_call" | custom-call | tf_op jit(solution)/shard_map/climb/pallas_call | solution.py:285
  20.6 1.6 %collective-permute-start.5 = (bf16[96,256]{1,0:T(8,128)(2,1)S(1)}, bf16[96,256]{1,0:T(8,128)(2,1)S(1)}, u32[]{:S(2)}, u32[]{:S(2)}) collective-permute-start(bf16[96,256]{1,0:T(8,128)(2,1)S(1)} %get-tuple-element.33.refs_13_.node), channel_id=1, source_target_pairs={{0,16},{1,129},{2,18},{3,147},{4,84},{5,213},{6,70},{7,199},{8,40}... | collective-permute-start | bytes 147464 | tf_op jit(solution)/shard_map/ppermute | solution.py:399
  22.2 1.7 %couple.1 = (f32[32,2048]{1,0:T(8,128)S(1)}, bf16[256,2048]{1,0:T(8,128)(2,1)S(1)}) custom-call(bf16[96,256]{1,0:T(8,128)(2,1)S(1)} %get-tuple-element.25.token.node.refs_0_, bf16[96,256]{1,0:T(8,128)(2,1)S(1)} %get-tuple-element.28.token.node.refs_1_, bf16[96,256]{1,0:T(8,128)(2,1)S(1)} %get-tuple-element.30.refs_1_.node.refs_2_, ...), custom_call_target="tpu_custom_call" | custom-call | flops 4000000000 | bytes 1000000 | tf_op jit(solution)/shard_map/couple/pallas_call | solution.py:319
  23.9 0.9 %collective-permute-done.5.source = bf16[96,256]{1,0:T(8,128)(2,1)S(1)} collective-permute-done((bf16[96,256]{1,0:T(8,128)(2,1)S(1)}, bf16[96,256]{1,0:T(8,128)(2,1)S(1)}, u32[]{:S(2)}, u32[]{:S(2)}) %collective-permute-start.5) | collective-permute-done | bytes 49184 | tf_op jit(solution)/shard_map/ppermute | solution.py:399
  24.8 0.4 top.1
  25.1 0.9 %collective-permute-start.6 = (f32[32,256]{1,0:T(8,128)S(1)}, f32[32,256]{1,0:T(8,128)S(1)}, u32[]{:S(2)}, u32[]{:S(2)}) collective-permute-start(f32[32,256]{1,0:T(8,128)S(1)} %top.1), channel_id=1, source_target_pairs={{0,1},{1,0},{2,3},{3,2},{4,5},{5,4},{6,7},{7,6},{8,9},{9,8},{10,11... | collective-permute-start | bytes 98312 | tf_op jit(solution)/shard_map/ppermute | solution.py:399
  26.0 0.2 collective-permute-done.8.block
  26.2 0.0 collective-permute-start.10
  26.2 2.5 %collective-permute-start.12 = (bf16[96,2048]{1,0:T(8,128)(2,1)S(1)}, bf16[96,2048]{1,0:T(8,128)(2,1)S(1)}, u32[]{:S(2)}, u32[]{:S(2)}) collective-permute-start(bf16[96,2048]{1,0:T(8,128)(2,1)S(1)} %get-tuple-element.40.block), channel_id=1, source_target_pairs={{0,2},{1,0},{2,4},{3,1},{4,6},{5,3},{6,8},{7,5},{8,10},{9,7},{10,1... | collective-permute-start | bytes 1179656 | tf_op jit(solution)/shard_map/ppermute | solution.py:399
  28.6 0.0 collective-permute-done.6
  28.6 2.2 %collective-permute-start.7 = (f32[32,256]{1,0:T(8,128)S(1)}, f32[32,256]{1,0:T(8,128)S(1)}, u32[]{:S(2)}, u32[]{:S(2)}) collective-permute-start(f32[32,256]{1,0:T(8,128)S(1)} %add.9.refs_1_), channel_id=1, source_target_pairs={{0,8},{1,9},{2,10},{3,11},{4,12},{5,13},{6,14},{7,15},{8,0},{9,1},... | collective-permute-start | bytes 98312 | tf_op jit(solution)/shard_map/ppermute | solution.py:399
  30.8 4.1 %near.5.refs_6_ = f32[32,2048]{1,0:T(8,128)S(1)} custom-call(s32[1,4]{1,0:T(1,128)S(1)} %copy-done.4, bf16[96,2048]{1,0:T(8,128)(2,1)S(1)} %collective-permute-done.8.block, bf16[80,2048]{1,0:T(8,128)(2,1)S(1)} %get-tuple-element.27.token.target.refs_0_, f32[32,256]{1,0:T(8,128)S(1)} %add.9.refs_1_), custom_call_target="tpu_custom_call" | custom-call | flops 4000000000 | bytes 1000000 | tf_op jit(solution)/shard_map/near/pallas_call | solution.py:211
  34.9 0.0 collective-permute-done.7
  35.0 1.2 %collective-permute-start.9 = (f32[32,256]{1,0:T(8,128)S(1)}, f32[32,256]{1,0:T(8,128)S(1)}, u32[]{:S(2)}, u32[]{:S(2)}) collective-permute-start(f32[32,256]{1,0:T(8,128)S(1)} %add.10.refs_1_), channel_id=1, source_target_pairs={{0,2},{1,3},{2,0},{3,1},{4,6},{5,7},{6,4},{7,5},{8,10},{9,11},{10,... | collective-permute-start | bytes 98312 | tf_op jit(solution)/shard_map/ppermute | solution.py:399
  36.1 0.0 collective-permute-done.10.block
  36.1 4.3 %near.6.refs_7_ = f32[32,2048]{1,0:T(8,128)S(1)} custom-call(s32[1,4]{1,0:T(1,128)S(1)} %copy-done.4, bf16[96,2048]{1,0:T(8,128)(2,1)S(1)} %collective-permute-done.10.block, bf16[80,2048]{1,0:T(8,128)(2,1)S(1)} %get-tuple-element.27.token.target.refs_0_, f32[32,256]{1,0:T(8,128)S(1)} %add.10.refs_1_), custom_call_target="tpu_custom_call" | custom-call | flops 500000000 | bytes 1000000 | tf_op jit(solution)/shard_map/near/pallas_call | solution.py:211
  40.5 0.0 collective-permute-done.9
  40.5 4.6 %collective-permute-start.11 = (f32[32,256]{1,0:T(8,128)S(1)}, f32[32,256]{1,0:T(8,128)S(1)}, u32[]{:S(2)}, u32[]{:S(2)}) collective-permute-start(f32[32,256]{1,0:T(8,128)S(1)} %add.11.refs_1_.refs_0_), channel_id=1, source_target_pairs={{0,6},{1,7},{2,4},{3,5},{4,2},{5,3},{6,0},{7,1},{8,14},{9,15},{10,... | collective-permute-start | bytes 98312 | tf_op jit(solution)/shard_map/ppermute | solution.py:399
  45.1 0.0 collective-permute-done.12.block
  45.1 4.1 %near.7.refs_8_ = f32[32,2048]{1,0:T(8,128)S(1)} custom-call(s32[1,4]{1,0:T(1,128)S(1)} %copy-done.4, bf16[96,2048]{1,0:T(8,128)(2,1)S(1)} %collective-permute-done.12.block, bf16[80,2048]{1,0:T(8,128)(2,1)S(1)} %get-tuple-element.27.token.target.refs_0_, f32[32,256]{1,0:T(8,128)S(1)} %add.11.refs_1_.refs_0_), custom_call_target="tpu_custom_call" | custom-call | flops 4000000000 | bytes 1000000 | tf_op jit(solution)/shard_map/near/pallas_call | solution.py:211
  49.2 0.0 collective-permute-done.11.refs_1_
  49.3 1.0 %down.1 = bf16[32,2048]{1,0:T(8,128)(2,1)} custom-call(f32[32,256]{1,0:T(8,128)S(1)} %add.11.refs_1_.refs_0_, f32[32,256]{1,0:T(8,128)S(1)} %collective-permute-done.11.refs_1_, f32[32,2048]{1,0:T(8,128)S(1)} %get-tuple-element.39.token.refs_2_, bf16[256,2048]{1,0:T(8,128)(2,1)S(1)} %get-tuple-element.44.refs_3_, f32[32,2048]{1,0:T(8,128)S(1)} %near_self.1.token.refs_4_, ...), custom_call_target="tpu_custom_call" | custom-call | tf_op jit(solution)/shard_map/down/pallas_call | solution.py:369
  (6 shorter events, 0.0 us)
Async XLA Ops:
  0.0 0.7 %copy-start.3 = (s32[1,256]{1,0:T(1,128)S(1)}, s32[1,256]{1,0:T(1,128)}, u32[]{:S(2)}) copy-start(s32[1,256]{1,0:T(1,128)} %skel.1) | copy-start | bytes 3076
  0.0 0.9 %copy-start.1 = (bf16[32,2048]{1,0:T(8,128)(2,1)S(1)}, bf16[32,2048]{1,0:T(8,128)(2,1)}, u32[]{:S(2)}) copy-start(bf16[32,2048]{1,0:T(8,128)(2,1)} %charges.1) | copy-start | bytes 393220
  0.0 1.0 %copy-start = (bf16[64,2048]{1,0:T(8,128)(2,1)S(1)}, bf16[64,2048]{1,0:T(8,128)(2,1)}, u32[]{:S(2)}) copy-start(bf16[64,2048]{1,0:T(8,128)(2,1)} %points.1) | copy-start | bytes 786436
  2.4 1.3 %collective-permute-start = (bf16[96,256]{1,0:T(8,128)(2,1)S(1)}, bf16[96,256]{1,0:T(8,128)(2,1)S(1)}, u32[]{:S(2)}, u32[]{:S(2)}) collective-permute-start(bf16[96,256]{1,0:T(8,128)(2,1)S(1)} %get-tuple-element.25.token.node.refs_0_), channel_id=1, source_target_pairs={{0,1},{1,0},{2,3},{3,2},{4,5},{5,4},{6,7},{7,6},{8,9},{9,8},{10,11... | collective-permute-start | bytes 147464 | tf_op jit(solution)/shard_map/ppermute | solution.py:399
  2.5 9.9 %collective-permute-start.3 = (bf16[96,2048]{1,0:T(8,128)(2,1)S(1)}, bf16[96,2048]{1,0:T(8,128)(2,1)S(1)}, u32[]{:S(2)}, u32[]{:S(2)}) collective-permute-start(bf16[96,2048]{1,0:T(8,128)(2,1)S(1)} %get-tuple-element.40.block), channel_id=1, source_target_pairs={{0,1},{1,0},{2,3},{3,2},{4,5},{5,4},{6,7},{7,6},{8,9},{9,8},{10,11... | collective-permute-start | bytes 1179656 | tf_op jit(solution)/shard_map/ppermute | solution.py:399
  3.0 0.7 %copy-start.2 = (s32[4,1,256]{2,1,0:T(1,128)S(1)}, s32[4,1,256]{2,1,0:T(1,128)}, u32[]{:S(2)}) copy-start(s32[4,1,256]{2,1,0:T(1,128)} %up.7) | copy-start | bytes 12292
  4.4 4.6 %collective-permute-start.1 = (bf16[96,256]{1,0:T(8,128)(2,1)S(1)}, bf16[96,256]{1,0:T(8,128)(2,1)S(1)}, u32[]{:S(2)}, u32[]{:S(2)}) collective-permute-start(bf16[96,256]{1,0:T(8,128)(2,1)S(1)} %get-tuple-element.28.token.node.refs_1_), channel_id=1, source_target_pairs={{0,2},{1,3},{2,0},{3,1},{4,6},{5,7},{6,4},{7,5},{8,10},{9,11},{10,... | collective-permute-start | bytes 147464 | tf_op jit(solution)/shard_map/ppermute | solution.py:399
  9.6 2.7 %copy-start.4 = (s32[1,4]{1,0:T(1,128)S(1)}, s32[1,4]{1,0:T(1,128)}, u32[]{:S(2)}) copy-start(s32[1,4]{1,0:T(1,128)} %mask.7) | copy-start | bytes 52
  9.6 5.4 %collective-permute-start.2 = (bf16[96,256]{1,0:T(8,128)(2,1)S(1)}, bf16[96,256]{1,0:T(8,128)(2,1)S(1)}, u32[]{:S(2)}, u32[]{:S(2)}) collective-permute-start(bf16[96,256]{1,0:T(8,128)(2,1)S(1)} %get-tuple-element.30.refs_1_.node.refs_2_), channel_id=1, source_target_pairs={{0,6},{1,7},{2,4},{3,5},{4,2},{5,3},{6,0},{7,1},{8,14},{9,15},{10,... | collective-permute-start | bytes 147464 | tf_op jit(solution)/shard_map/ppermute | solution.py:399
  15.7 4.2 %collective-permute-start.4 = (bf16[96,256]{1,0:T(8,128)(2,1)S(1)}, bf16[96,256]{1,0:T(8,128)(2,1)S(1)}, u32[]{:S(2)}, u32[]{:S(2)}) collective-permute-start(bf16[96,256]{1,0:T(8,128)(2,1)S(1)} %get-tuple-element.32.node.token.refs_3_), channel_id=1, source_target_pairs={{0,8},{1,9},{2,10},{3,11},{4,12},{5,13},{6,14},{7,15},{8,0},{9,1},... | collective-permute-start | bytes 147464 | tf_op jit(solution)/shard_map/ppermute | solution.py:399
  16.6 9.5 %collective-permute-start.8 = (bf16[96,2048]{1,0:T(8,128)(2,1)S(1)}, bf16[96,2048]{1,0:T(8,128)(2,1)S(1)}, u32[]{:S(2)}, u32[]{:S(2)}) collective-permute-start(bf16[96,2048]{1,0:T(8,128)(2,1)S(1)} %get-tuple-element.40.block), channel_id=1, source_target_pairs={{0,255},{1,2},{2,1},{3,4},{4,3},{5,6},{6,5},{7,8},{8,7},{9,10},{10... | collective-permute-start | bytes 1179656 | tf_op jit(solution)/shard_map/ppermute | solution.py:399
  20.6 4.2 %collective-permute-start.5 = (bf16[96,256]{1,0:T(8,128)(2,1)S(1)}, bf16[96,256]{1,0:T(8,128)(2,1)S(1)}, u32[]{:S(2)}, u32[]{:S(2)}) collective-permute-start(bf16[96,256]{1,0:T(8,128)(2,1)S(1)} %get-tuple-element.33.refs_13_.node), channel_id=1, source_target_pairs={{0,16},{1,129},{2,18},{3,147},{4,84},{5,213},{6,70},{7,199},{8,40}... | collective-permute-start | bytes 147464 | tf_op jit(solution)/shard_map/ppermute | solution.py:399
  25.1 3.5 %collective-permute-start.6 = (f32[32,256]{1,0:T(8,128)S(1)}, f32[32,256]{1,0:T(8,128)S(1)}, u32[]{:S(2)}, u32[]{:S(2)}) collective-permute-start(f32[32,256]{1,0:T(8,128)S(1)} %top.1), channel_id=1, source_target_pairs={{0,1},{1,0},{2,3},{3,2},{4,5},{5,4},{6,7},{7,6},{8,9},{9,8},{10,11... | collective-permute-start | bytes 98312 | tf_op jit(solution)/shard_map/ppermute | solution.py:399
  26.2 10.0 %collective-permute-start.10 = (bf16[96,2048]{1,0:T(8,128)(2,1)S(1)}, bf16[96,2048]{1,0:T(8,128)(2,1)S(1)}, u32[]{:S(2)}, u32[]{:S(2)}) collective-permute-start(bf16[96,2048]{1,0:T(8,128)(2,1)S(1)} %collective-permute-done.8.block), channel_id=1, source_target_pairs={{0,1},{1,0},{2,3},{3,2},{4,5},{5,4},{6,7},{7,6},{8,9},{9,8},{10,11... | collective-permute-start | bytes 1179656 | tf_op jit(solution)/shard_map/ppermute | solution.py:399
  26.2 18.9 %collective-permute-start.12 = (bf16[96,2048]{1,0:T(8,128)(2,1)S(1)}, bf16[96,2048]{1,0:T(8,128)(2,1)S(1)}, u32[]{:S(2)}, u32[]{:S(2)}) collective-permute-start(bf16[96,2048]{1,0:T(8,128)(2,1)S(1)} %get-tuple-element.40.block), channel_id=1, source_target_pairs={{0,2},{1,0},{2,4},{3,1},{4,6},{5,3},{6,8},{7,5},{8,10},{9,7},{10,1... | collective-permute-start | bytes 1179656 | tf_op jit(solution)/shard_map/ppermute | solution.py:399
  28.6 6.3 %collective-permute-start.7 = (f32[32,256]{1,0:T(8,128)S(1)}, f32[32,256]{1,0:T(8,128)S(1)}, u32[]{:S(2)}, u32[]{:S(2)}) collective-permute-start(f32[32,256]{1,0:T(8,128)S(1)} %add.9.refs_1_), channel_id=1, source_target_pairs={{0,8},{1,9},{2,10},{3,11},{4,12},{5,13},{6,14},{7,15},{8,0},{9,1},... | collective-permute-start | bytes 98312 | tf_op jit(solution)/shard_map/ppermute | solution.py:399
  35.0 5.5 %collective-permute-start.9 = (f32[32,256]{1,0:T(8,128)S(1)}, f32[32,256]{1,0:T(8,128)S(1)}, u32[]{:S(2)}, u32[]{:S(2)}) collective-permute-start(f32[32,256]{1,0:T(8,128)S(1)} %add.10.refs_1_), channel_id=1, source_target_pairs={{0,2},{1,3},{2,0},{3,1},{4,6},{5,7},{6,4},{7,5},{8,10},{9,11},{10,... | collective-permute-start | bytes 98312 | tf_op jit(solution)/shard_map/ppermute | solution.py:399
  40.5 8.7 %collective-permute-start.11 = (f32[32,256]{1,0:T(8,128)S(1)}, f32[32,256]{1,0:T(8,128)S(1)}, u32[]{:S(2)}, u32[]{:S(2)}) collective-permute-start(f32[32,256]{1,0:T(8,128)S(1)} %add.11.refs_1_.refs_0_), channel_id=1, source_target_pairs={{0,6},{1,7},{2,4},{3,5},{4,2},{5,3},{6,0},{7,1},{8,14},{9,15},{10,... | collective-permute-start | bytes 98312 | tf_op jit(solution)/shard_map/ppermute | solution.py:399

commit v3 on v2

--- a/solution.py
+++ b/solution.py
@@ -424,7 +424,7 @@
     pieces.append((0, token))
     node = step(2, token)
     exchange(6)
-    token = piece(0, 0, 2048, mate, None, node)
+    token = piece(0, 0, 1280, mate, None, node)
     node = step(3, token)
     exchange(8)
     sent = after(block, node)
@@ -434,7 +434,8 @@
     constant, whole = couple(nodes, partners, halves, weights_t, node)
     arrived = send(node, top_target)
     passed = send(after(across, node), lambda i: i ^ 1)
-    wave = top(levels, node, arrived, constant)
+    token = piece(0, 1280, 768, mate, None, constant)
+    wave = top(levels, node, arrived, token)
     arrived = send(wave, lambda i: i ^ 1)
     wave = wave + arrived
     arrived = send(wave, lambda i: i ^ 8)

time: 50.7 us -> 50.2 us (level)
  the two profiles are of different devices: /device:TPU:102 before, /device:TPU:2 now
where the time goes in v3:
time: 50.2 us; the launch traced here: 50.5 us
  starting transfers between devices  22.7 us (45%)
  Pallas kernels  20.6 us (41%)
  waiting for transfers between devices  6.02 us (12%)
  local copies, waits for them, and re-layouts  1.03 us (2%)
    ppermute x13, starting transfers between devices, send(): return lax.ppermute(value, 'leaf', pairs)  22.7 us
    pallas_call x5, Pallas kernels, near(): pl.pallas_call(functools.partial(near_kernel, place, (first, width), fres...  10.4 us
    ppermute x13, waiting for transfers between devices, send(): return lax.ppermute(value, 'leaf', pairs)  6.02 us
    pallas_call x1, Pallas kernels, near_self(): pl.pallas_call(self_kernel, out_shape=jax.ShapeDtypeStruct((block.shape[0...  2.9 us
    pallas_call x4, Pallas kernels, climb(): pl.pallas_call(functools.partial(level_kernel, level), out_shape=(jax.Sha...  2.68 us
    pallas_call x1, Pallas kernels, couple(): pl.pallas_call(functools.partial(couple_kernel, levels), out_shape=(jax.S...  1.68 us
    pallas_call x1, Pallas kernels, leaf(): pl.pallas_call(leaf_kernel, out_shape=(jax.ShapeDtypeStruct((rank, count)...  1.36 us
    unnamed x10, local copies, waits for them, and re-layouts  1.03 us
  transfers between devices with their start and end apart: 13, of which 5 were waited for; matrix products, arithmetic and copies ran while one was open for 0% of the time, Pallas kernels for 35%

profile of v3, /device:TPU:2, one launch (start us, length us, event | category | flops | bytes accessed | tf_op | source)
XLA Modules:
  0.0 50.5 jit_solution(15124109214093353665)
XLA Ops:
  0.0 0.0 copy-start.3
  0.0 0.7 %copy-done.3 = s32[1,256]{1,0:T(1,128)S(1)} copy-done((s32[1,256]{1,0:T(1,128)S(1)}, s32[1,256]{1,0:T(1,128)}, u32[]{:S(2)}) %copy-start.3) | copy-done | bytes 1048
  0.7 0.2 copy-done.1
  0.9 0.1 copy-done
  1.0 1.4 %leaf.1 = (bf16[256,2048]{1,0:T(8,128)(2,1)S(1)}, bf16[96,256]{1,0:T(8,128)(2,1)S(1)}, bf16[96,2048]{1,0:T(8,128)(2,1)S(1)}) custom-call(bf16[64,2048]{1,0:T(8,128)(2,1)S(1)} %copy-done, bf16[32,2048]{1,0:T(8,128)(2,1)S(1)} %copy-done.1, s32[1,256]{1,0:T(1,128)S(1)} %copy-done.3, f32[8,128]{1,0:T(8,128)S(1)} %first.1.token), custom_call_target="tpu_custom_call" | custom-call | tf_op jit(solution)/shard_map/leaf/pallas_call | solution.py:112
  2.4 0.1 collective-permute-start
  2.5 0.5 collective-permute-start.3
  3.0 0.3 prep.1
  3.2 0.5 collective-permute-done.partner.refs_4_
  3.7 0.0 copy-done.2
  3.7 0.7 %climb.4 = (bf16[256,256]{1,0:T(8,128)(2,1)S(1)}, bf16[96,256]{1,0:T(8,128)(2,1)S(1)}) custom-call(s32[4,1,256]{2,1,0:T(1,128)S(1)} %copy-done.2, bf16[96,256]{1,0:T(8,128)(2,1)S(1)} %get-tuple-element.25.token.node.refs_0_, bf16[96,256]{1,0:T(8,128)(2,1)S(1)} %collective-permute-done.partner.refs_4_, bf16[80,2048]{1,0:T(8,128)(2,1)S(1)} %get-tuple-element.27.token.target.refs_0_), custom_call_target="tpu_custom_call" | custom-call | tf_op jit(solution)/shard_map/climb/pallas_call | solution.py:285
  4.4 1.7 %collective-permute-start.1 = (bf16[96,256]{1,0:T(8,128)(2,1)S(1)}, bf16[96,256]{1,0:T(8,128)(2,1)S(1)}, u32[]{:S(2)}, u32[]{:S(2)}) collective-permute-start(bf16[96,256]{1,0:T(8,128)(2,1)S(1)} %get-tuple-element.28.token.node.refs_1_), channel_id=1, source_target_pairs={{0,2},{1,3},{2,0},{3,1},{4,6},{5,7},{6,4},{7,5},{8,10},{9,11},{10,... | collective-permute-start | bytes 147464 | tf_op jit(solution)/shard_map/ppermute | solution.py:399
  6.0 2.9 %near_self.1.token.refs_4_ = f32[32,2048]{1,0:T(8,128)S(1)} custom-call(bf16[96,2048]{1,0:T(8,128)(2,1)S(1)} %get-tuple-element.40.block, bf16[2048,128]{1,0:T(8,128)(2,1)S(1)} %get-tuple-element.29.source, bf16[80,2048]{1,0:T(8,128)(2,1)S(1)} %get-tuple-element.27.token.target.refs_0_, bf16[96,256]{1,0:T(8,128)(2,1)S(1)} %get-tuple-element.28.token.node.refs_1_), custom_call_target="tpu_custom_call" | custom-call | flops 4000000000 | bytes 1000000 | tf_op jit(solution)/shard_map/near_self/pallas_call | solution.py:250
  8.9 0.0 collective-permute-done.1.partner.refs_5_
  9.0 0.7 %climb.5 = (bf16[256,256]{1,0:T(8,128)(2,1)S(1)}, bf16[96,256]{1,0:T(8,128)(2,1)S(1)}) custom-call(s32[4,1,256]{2,1,0:T(1,128)S(1)} %copy-done.2, bf16[96,256]{1,0:T(8,128)(2,1)S(1)} %get-tuple-element.28.token.node.refs_1_, bf16[96,256]{1,0:T(8,128)(2,1)S(1)} %collective-permute-done.1.partner.refs_5_, f32[32,2048]{1,0:T(8,128)S(1)} %near_self.1.token.refs_4_), custom_call_target="tpu_custom_call" | custom-call | tf_op jit(solution)/shard_map/climb/pallas_call | solution.py:285
  9.6 0.0 copy-start.4
  9.6 2.7 %collective-permute-start.2 = (bf16[96,256]{1,0:T(8,128)(2,1)S(1)}, bf16[96,256]{1,0:T(8,128)(2,1)S(1)}, u32[]{:S(2)}, u32[]{:S(2)}) collective-permute-start(bf16[96,256]{1,0:T(8,128)(2,1)S(1)} %get-tuple-element.30.refs_1_.node.refs_2_), channel_id=1, source_target_pairs={{0,6},{1,7},{2,4},{3,5},{4,2},{5,3},{6,0},{7,1},{8,14},{9,15},{10,... | collective-permute-start | bytes 147464 | tf_op jit(solution)/shard_map/ppermute | solution.py:399
  12.4 0.0 collective-permute-done.3.block
  12.4 0.0 copy-done.4
  12.4 2.9 %near.5.token.refs_5_ = f32[32,1280]{1,0:T(8,128)S(1)} custom-call(s32[1,4]{1,0:T(1,128)S(1)} %copy-done.4, bf16[96,2048]{1,0:T(8,128)(2,1)S(1)} %collective-permute-done.3.block, bf16[80,2048]{1,0:T(8,128)(2,1)S(1)} %get-tuple-element.27.token.target.refs_0_, bf16[96,256]{1,0:T(8,128)(2,1)S(1)} %get-tuple-element.30.refs_1_.node.refs_2_), custom_call_target="tpu_custom_call" | custom-call | flops 2500000000 | bytes 1000000 | tf_op jit(solution)/shard_map/near/pallas_call | solution.py:211
  15.2 0.0 collective-permute-done.2.partner.refs_6_
  15.2 0.7 %climb.6 = (bf16[256,256]{1,0:T(8,128)(2,1)S(1)}, bf16[96,256]{1,0:T(8,128)(2,1)S(1)}) custom-call(s32[4,1,256]{2,1,0:T(1,128)S(1)} %copy-done.2, bf16[96,256]{1,0:T(8,128)(2,1)S(1)} %get-tuple-element.30.refs_1_.node.refs_2_, bf16[96,256]{1,0:T(8,128)(2,1)S(1)} %collective-permute-done.2.partner.refs_6_, f32[32,1280]{1,0:T(8,128)S(1)} %near.5.token.refs_5_), custom_call_target="tpu_custom_call" | custom-call | tf_op jit(solution)/shard_map/climb/pallas_call | solution.py:285
  15.9 1.8 %collective-permute-start.4 = (bf16[96,256]{1,0:T(8,128)(2,1)S(1)}, bf16[96,256]{1,0:T(8,128)(2,1)S(1)}, u32[]{:S(2)}, u32[]{:S(2)}) collective-permute-start(bf16[96,256]{1,0:T(8,128)(2,1)S(1)} %get-tuple-element.32.node.token.refs_3_), channel_id=1, source_target_pairs={{0,8},{1,9},{2,10},{3,11},{4,12},{5,13},{6,14},{7,15},{8,0},{9,1},... | collective-permute-start | bytes 147464 | tf_op jit(solution)/shard_map/ppermute | solution.py:399
  17.7 0.0 collective-permute-start.8
  17.7 2.4 %collective-permute-done.4.partner.refs_7_ = bf16[96,256]{1,0:T(8,128)(2,1)S(1)} collective-permute-done((bf16[96,256]{1,0:T(8,128)(2,1)S(1)}, bf16[96,256]{1,0:T(8,128)(2,1)S(1)}, u32[]{:S(2)}, u32[]{:S(2)}) %collective-permute-start.4) | collective-permute-done | bytes 49184 | tf_op jit(solution)/shard_map/ppermute | solution.py:399
  20.1 0.7 %climb.7 = (bf16[256,256]{1,0:T(8,128)(2,1)S(1)}, bf16[96,256]{1,0:T(8,128)(2,1)S(1)}) custom-call(s32[4,1,256]{2,1,0:T(1,128)S(1)} %copy-done.2, bf16[96,256]{1,0:T(8,128)(2,1)S(1)} %get-tuple-element.32.node.token.refs_3_, bf16[96,256]{1,0:T(8,128)(2,1)S(1)} %collective-permute-done.4.partner.refs_7_, bf16[96,256]{1,0:T(8,128)(2,1)S(1)} %get-tuple-element.32.node.token.refs_3_), custom_call_target="tpu_custom_call" | custom-call | tf_op jit(solution)/shard_map/climb/pallas_call | solution.py:285
  20.8 2.2 %collective-permute-start.5 = (bf16[96,256]{1,0:T(8,128)(2,1)S(1)}, bf16[96,256]{1,0:T(8,128)(2,1)S(1)}, u32[]{:S(2)}, u32[]{:S(2)}) collective-permute-start(bf16[96,256]{1,0:T(8,128)(2,1)S(1)} %get-tuple-element.33.refs_13_.node), channel_id=1, source_target_pairs={{0,16},{1,129},{2,18},{3,147},{4,84},{5,213},{6,70},{7,199},{8,40}... | collective-permute-start | bytes 147464 | tf_op jit(solution)/shard_map/ppermute | solution.py:399
  23.0 1.7 %couple.1 = (f32[32,2048]{1,0:T(8,128)S(1)}, bf16[256,2048]{1,0:T(8,128)(2,1)S(1)}) custom-call(bf16[96,256]{1,0:T(8,128)(2,1)S(1)} %get-tuple-element.25.token.node.refs_0_, bf16[96,256]{1,0:T(8,128)(2,1)S(1)} %get-tuple-element.28.token.node.refs_1_, bf16[96,256]{1,0:T(8,128)(2,1)S(1)} %get-tuple-element.30.refs_1_.node.refs_2_, ...), custom_call_target="tpu_custom_call" | custom-call | flops 4000000000 | bytes 1000000 | tf_op jit(solution)/shard_map/couple/pallas_call | solution.py:319
  24.6 2.0 %near.6.token.refs_6_ = f32[32,768]{1,0:T(8,128)S(1)} custom-call(s32[1,4]{1,0:T(1,128)S(1)} %copy-done.4, bf16[96,2048]{1,0:T(8,128)(2,1)S(1)} %collective-permute-done.3.block, bf16[80,2048]{1,0:T(8,128)(2,1)S(1)} %get-tuple-element.27.token.target.refs_0_, f32[32,2048]{1,0:T(8,128)S(1)} %get-tuple-element.39.refs_1_.refs_2_), custom_call_target="tpu_custom_call" | custom-call | flops 1500000000 | bytes 1000000 | tf_op jit(solution)/shard_map/near/pallas_call | solution.py:211
  26.7 0.0 collective-permute-done.5.source
  26.7 0.4 top.1
  27.1 2.6 %collective-permute-start.6 = (f32[32,256]{1,0:T(8,128)S(1)}, f32[32,256]{1,0:T(8,128)S(1)}, u32[]{:S(2)}, u32[]{:S(2)}) collective-permute-start(f32[32,256]{1,0:T(8,128)S(1)} %top.1), channel_id=1, source_target_pairs={{0,1},{1,0},{2,3},{3,2},{4,5},{5,4},{6,7},{7,6},{8,9},{9,8},{10,11... | collective-permute-start | bytes 98312 | tf_op jit(solution)/shard_map/ppermute | solution.py:399
  29.7 0.0 collective-permute-done.8.block
  29.7 0.1 collective-permute-start.10
  29.8 0.4 collective-permute-start.12
  30.1 0.4 collective-permute-done.6
  30.5 2.5 %collective-permute-start.7 = (f32[32,256]{1,0:T(8,128)S(1)}, f32[32,256]{1,0:T(8,128)S(1)}, u32[]{:S(2)}, u32[]{:S(2)}) collective-permute-start(f32[32,256]{1,0:T(8,128)S(1)} %add.9.refs_1_), channel_id=1, source_target_pairs={{0,8},{1,9},{2,10},{3,11},{4,12},{5,13},{6,14},{7,15},{8,0},{9,1},... | collective-permute-start | bytes 98312 | tf_op jit(solution)/shard_map/ppermute | solution.py:399
  33.0 0.6 %near.7.refs_7_ = f32[32,2048]{1,0:T(8,128)S(1)} custom-call(s32[1,4]{1,0:T(1,128)S(1)} %copy-done.4, bf16[96,2048]{1,0:T(8,128)(2,1)S(1)} %collective-permute-done.8.block, bf16[80,2048]{1,0:T(8,128)(2,1)S(1)} %get-tuple-element.27.token.target.refs_0_, f32[32,256]{1,0:T(8,128)S(1)} %add.9.refs_1_), custom_call_target="tpu_custom_call" | custom-call | flops 4000000000 | bytes 1000000 | tf_op jit(solution)/shard_map/near/pallas_call | solution.py:211
  33.6 1.3 %collective-permute-done.7 = f32[32,256]{1,0:T(8,128)S(1)} collective-permute-done((f32[32,256]{1,0:T(8,128)S(1)}, f32[32,256]{1,0:T(8,128)S(1)}, u32[]{:S(2)}, u32[]{:S(2)}) %collective-permute-start.7) | collective-permute-done | bytes 32800 | tf_op jit(solution)/shard_map/ppermute | solution.py:399
  34.9 3.3 %collective-permute-start.9 = (f32[32,256]{1,0:T(8,128)S(1)}, f32[32,256]{1,0:T(8,128)S(1)}, u32[]{:S(2)}, u32[]{:S(2)}) collective-permute-start(f32[32,256]{1,0:T(8,128)S(1)} %add.10.refs_1_), channel_id=1, source_target_pairs={{0,2},{1,3},{2,0},{3,1},{4,6},{5,7},{6,4},{7,5},{8,10},{9,11},{10,... | collective-permute-start | bytes 98312 | tf_op jit(solution)/shard_map/ppermute | solution.py:399
  38.2 0.0 collective-permute-done.10.block
  38.2 0.8 %near.8.refs_8_ = f32[32,2048]{1,0:T(8,128)S(1)} custom-call(s32[1,4]{1,0:T(1,128)S(1)} %copy-done.4, bf16[96,2048]{1,0:T(8,128)(2,1)S(1)} %collective-permute-done.10.block, bf16[80,2048]{1,0:T(8,128)(2,1)S(1)} %get-tuple-element.27.token.target.refs_0_, f32[32,256]{1,0:T(8,128)S(1)} %add.10.refs_1_), custom_call_target="tpu_custom_call" | custom-call | flops 500000000 | bytes 1000000 | tf_op jit(solution)/shard_map/near/pallas_call | solution.py:211
  39.0 1.4 %collective-permute-done.9 = f32[32,256]{1,0:T(8,128)S(1)} collective-permute-done((f32[32,256]{1,0:T(8,128)S(1)}, f32[32,256]{1,0:T(8,128)S(1)}, u32[]{:S(2)}, u32[]{:S(2)}) %collective-permute-start.9) | collective-permute-done | bytes 32800 | tf_op jit(solution)/shard_map/ppermute | solution.py:399
  40.4 5.0 %collective-permute-start.11 = (f32[32,256]{1,0:T(8,128)S(1)}, f32[32,256]{1,0:T(8,128)S(1)}, u32[]{:S(2)}, u32[]{:S(2)}) collective-permute-start(f32[32,256]{1,0:T(8,128)S(1)} %add.11.refs_1_.refs_0_), channel_id=1, source_target_pairs={{0,6},{1,7},{2,4},{3,5},{4,2},{5,3},{6,0},{7,1},{8,14},{9,15},{10,... | collective-permute-start | bytes 98312 | tf_op jit(solution)/shard_map/ppermute | solution.py:399
  45.4 0.0 collective-permute-done.12.block
  45.4 4.1 %near.9.refs_9_ = f32[32,2048]{1,0:T(8,128)S(1)} custom-call(s32[1,4]{1,0:T(1,128)S(1)} %copy-done.4, bf16[96,2048]{1,0:T(8,128)(2,1)S(1)} %collective-permute-done.12.block, bf16[80,2048]{1,0:T(8,128)(2,1)S(1)} %get-tuple-element.27.token.target.refs_0_, f32[32,256]{1,0:T(8,128)S(1)} %add.11.refs_1_.refs_0_), custom_call_target="tpu_custom_call" | custom-call | flops 4000000000 | bytes 1000000 | tf_op jit(solution)/shard_map/near/pallas_call | solution.py:211
  49.6 0.0 collective-permute-done.11.refs_1_
  49.6 1.0 %down.1 = bf16[32,2048]{1,0:T(8,128)(2,1)} custom-call(f32[32,256]{1,0:T(8,128)S(1)} %add.11.refs_1_.refs_0_, f32[32,256]{1,0:T(8,128)S(1)} %collective-permute-done.11.refs_1_, f32[32,2048]{1,0:T(8,128)S(1)} %get-tuple-element.39.refs_1_.refs_2_, bf16[256,2048]{1,0:T(8,128)(2,1)S(1)} %get-tuple-element.44.refs_3_, f32[32,2048]{1,0:T(8,128)S(1)} %near_self.1.token.refs_4_, ...), custom_call_target="tpu_custom_call" | custom-call | tf_op jit(solution)/shard_map/down/pallas_call | solution.py:369
  (7 shorter events, 0.0 us)
Async XLA Ops:
  0.0 0.7 %copy-start.3 = (s32[1,256]{1,0:T(1,128)S(1)}, s32[1,256]{1,0:T(1,128)}, u32[]{:S(2)}) copy-start(s32[1,256]{1,0:T(1,128)} %skel.1) | copy-start | bytes 3076
  0.0 0.9 %copy-start.1 = (bf16[32,2048]{1,0:T(8,128)(2,1)S(1)}, bf16[32,2048]{1,0:T(8,128)(2,1)}, u32[]{:S(2)}) copy-start(bf16[32,2048]{1,0:T(8,128)(2,1)} %charges.1) | copy-start | bytes 393220
  0.0 1.0 %copy-start = (bf16[64,2048]{1,0:T(8,128)(2,1)S(1)}, bf16[64,2048]{1,0:T(8,128)(2,1)}, u32[]{:S(2)}) copy-start(bf16[64,2048]{1,0:T(8,128)(2,1)} %points.1) | copy-start | bytes 786436
  2.4 1.3 %collective-permute-start = (bf16[96,256]{1,0:T(8,128)(2,1)S(1)}, bf16[96,256]{1,0:T(8,128)(2,1)S(1)}, u32[]{:S(2)}, u32[]{:S(2)}) collective-permute-start(bf16[96,256]{1,0:T(8,128)(2,1)S(1)} %get-tuple-element.25.token.node.refs_0_), channel_id=1, source_target_pairs={{0,1},{1,0},{2,3},{3,2},{4,5},{5,4},{6,7},{7,6},{8,9},{9,8},{10,11... | collective-permute-start | bytes 147464 | tf_op jit(solution)/shard_map/ppermute | solution.py:399
  2.5 9.9 %collective-permute-start.3 = (bf16[96,2048]{1,0:T(8,128)(2,1)S(1)}, bf16[96,2048]{1,0:T(8,128)(2,1)S(1)}, u32[]{:S(2)}, u32[]{:S(2)}) collective-permute-start(bf16[96,2048]{1,0:T(8,128)(2,1)S(1)} %get-tuple-element.40.block), channel_id=1, source_target_pairs={{0,1},{1,0},{2,3},{3,2},{4,5},{5,4},{6,7},{7,6},{8,9},{9,8},{10,11... | collective-permute-start | bytes 1179656 | tf_op jit(solution)/shard_map/ppermute | solution.py:399
  3.0 0.7 %copy-start.2 = (s32[4,1,256]{2,1,0:T(1,128)S(1)}, s32[4,1,256]{2,1,0:T(1,128)}, u32[]{:S(2)}) copy-start(s32[4,1,256]{2,1,0:T(1,128)} %up.7) | copy-start | bytes 12292
  4.4 4.6 %collective-permute-start.1 = (bf16[96,256]{1,0:T(8,128)(2,1)S(1)}, bf16[96,256]{1,0:T(8,128)(2,1)S(1)}, u32[]{:S(2)}, u32[]{:S(2)}) collective-permute-start(bf16[96,256]{1,0:T(8,128)(2,1)S(1)} %get-tuple-element.28.token.node.refs_1_), channel_id=1, source_target_pairs={{0,2},{1,3},{2,0},{3,1},{4,6},{5,7},{6,4},{7,5},{8,10},{9,11},{10,... | collective-permute-start | bytes 147464 | tf_op jit(solution)/shard_map/ppermute | solution.py:399
  9.6 2.7 %copy-start.4 = (s32[1,4]{1,0:T(1,128)S(1)}, s32[1,4]{1,0:T(1,128)}, u32[]{:S(2)}) copy-start(s32[1,4]{1,0:T(1,128)} %mask.9) | copy-start | bytes 52
  9.6 5.6 %collective-permute-start.2 = (bf16[96,256]{1,0:T(8,128)(2,1)S(1)}, bf16[96,256]{1,0:T(8,128)(2,1)S(1)}, u32[]{:S(2)}, u32[]{:S(2)}) collective-permute-start(bf16[96,256]{1,0:T(8,128)(2,1)S(1)} %get-tuple-element.30.refs_1_.node.refs_2_), channel_id=1, source_target_pairs={{0,6},{1,7},{2,4},{3,5},{4,2},{5,3},{6,0},{7,1},{8,14},{9,15},{10,... | collective-permute-start | bytes 147464 | tf_op jit(solution)/shard_map/ppermute | solution.py:399
  15.9 4.2 %collective-permute-start.4 = (bf16[96,256]{1,0:T(8,128)(2,1)S(1)}, bf16[96,256]{1,0:T(8,128)(2,1)S(1)}, u32[]{:S(2)}, u32[]{:S(2)}) collective-permute-start(bf16[96,256]{1,0:T(8,128)(2,1)S(1)} %get-tuple-element.32.node.token.refs_3_), channel_id=1, source_target_pairs={{0,8},{1,9},{2,10},{3,11},{4,12},{5,13},{6,14},{7,15},{8,0},{9,1},... | collective-permute-start | bytes 147464 | tf_op jit(solution)/shard_map/ppermute | solution.py:399
  17.7 12.0 %collective-permute-start.8 = (bf16[96,2048]{1,0:T(8,128)(2,1)S(1)}, bf16[96,2048]{1,0:T(8,128)(2,1)S(1)}, u32[]{:S(2)}, u32[]{:S(2)}) collective-permute-start(bf16[96,2048]{1,0:T(8,128)(2,1)S(1)} %get-tuple-element.40.block), channel_id=1, source_target_pairs={{0,255},{1,2},{2,1},{3,4},{4,3},{5,6},{6,5},{7,8},{8,7},{9,10},{10... | collective-permute-start | bytes 1179656 | tf_op jit(solution)/shard_map/ppermute | solution.py:399
  20.8 5.9 %collective-permute-start.5 = (bf16[96,256]{1,0:T(8,128)(2,1)S(1)}, bf16[96,256]{1,0:T(8,128)(2,1)S(1)}, u32[]{:S(2)}, u32[]{:S(2)}) collective-permute-start(bf16[96,256]{1,0:T(8,128)(2,1)S(1)} %get-tuple-element.33.refs_13_.node), channel_id=1, source_target_pairs={{0,16},{1,129},{2,18},{3,147},{4,84},{5,213},{6,70},{7,199},{8,40}... | collective-permute-start | bytes 147464 | tf_op jit(solution)/shard_map/ppermute | solution.py:399
  27.1 3.4 %collective-permute-start.6 = (f32[32,256]{1,0:T(8,128)S(1)}, f32[32,256]{1,0:T(8,128)S(1)}, u32[]{:S(2)}, u32[]{:S(2)}) collective-permute-start(f32[32,256]{1,0:T(8,128)S(1)} %top.1), channel_id=1, source_target_pairs={{0,1},{1,0},{2,3},{3,2},{4,5},{5,4},{6,7},{7,6},{8,9},{9,8},{10,11... | collective-permute-start | bytes 98312 | tf_op jit(solution)/shard_map/ppermute | solution.py:399
  29.7 8.5 %collective-permute-start.10 = (bf16[96,2048]{1,0:T(8,128)(2,1)S(1)}, bf16[96,2048]{1,0:T(8,128)(2,1)S(1)}, u32[]{:S(2)}, u32[]{:S(2)}) collective-permute-start(bf16[96,2048]{1,0:T(8,128)(2,1)S(1)} %collective-permute-done.8.block), channel_id=1, source_target_pairs={{0,1},{1,0},{2,3},{3,2},{4,5},{5,4},{6,7},{7,6},{8,9},{9,8},{10,11... | collective-permute-start | bytes 1179656 | tf_op jit(solution)/shard_map/ppermute | solution.py:399
  29.8 15.7 %collective-permute-start.12 = (bf16[96,2048]{1,0:T(8,128)(2,1)S(1)}, bf16[96,2048]{1,0:T(8,128)(2,1)S(1)}, u32[]{:S(2)}, u32[]{:S(2)}) collective-permute-start(bf16[96,2048]{1,0:T(8,128)(2,1)S(1)} %get-tuple-element.40.block), channel_id=1, source_target_pairs={{0,2},{1,0},{2,4},{3,1},{4,6},{5,3},{6,8},{7,5},{8,10},{9,7},{10,1... | collective-permute-start | bytes 1179656 | tf_op jit(solution)/shard_map/ppermute | solution.py:399
  30.5 4.4 %collective-permute-start.7 = (f32[32,256]{1,0:T(8,128)S(1)}, f32[32,256]{1,0:T(8,128)S(1)}, u32[]{:S(2)}, u32[]{:S(2)}) collective-permute-start(f32[32,256]{1,0:T(8,128)S(1)} %add.9.refs_1_), channel_id=1, source_target_pairs={{0,8},{1,9},{2,10},{3,11},{4,12},{5,13},{6,14},{7,15},{8,0},{9,1},... | collective-permute-start | bytes 98312 | tf_op jit(solution)/shard_map/ppermute | solution.py:399
  34.9 5.5 %collective-permute-start.9 = (f32[32,256]{1,0:T(8,128)S(1)}, f32[32,256]{1,0:T(8,128)S(1)}, u32[]{:S(2)}, u32[]{:S(2)}) collective-permute-start(f32[32,256]{1,0:T(8,128)S(1)} %add.10.refs_1_), channel_id=1, source_target_pairs={{0,2},{1,3},{2,0},{3,1},{4,6},{5,7},{6,4},{7,5},{8,10},{9,11},{10,... | collective-permute-start | bytes 98312 | tf_op jit(solution)/shard_map/ppermute | solution.py:399
  40.4 9.1 %collective-permute-start.11 = (f32[32,256]{1,0:T(8,128)S(1)}, f32[32,256]{1,0:T(8,128)S(1)}, u32[]{:S(2)}, u32[]{:S(2)}) collective-permute-start(f32[32,256]{1,0:T(8,128)S(1)} %add.11.refs_1_.refs_0_), channel_id=1, source_target_pairs={{0,6},{1,7},{2,4},{3,5},{4,2},{5,3},{6,0},{7,1},{8,14},{9,15},{10,... | collective-permute-start | bytes 98312 | tf_op jit(solution)/shard_map/ppermute | solution.py:399
